TPU v7x, 256 devices: a whole 4x4x8 slice. The times are simulated.
256 devices in a mesh: gx: 8 (over z), gy: 4 (over y_lo, core), gz: 8 (over x, y_hi).
Axes of the slice: x: 4, y: 4 (y_hi: 2, y_lo: 2; y = y_hi * 2 + y_lo), z: 8, core: 2. Of those that a mesh axis runs over, the one named last changes fastest.
Arguments:
- tokens: bfloat16 [768, 6144], P(('gy', 'gx'), 'gz'), may hold values from -6 to 6
- gain: float32 [6144], P('gz'), may hold values from 0.5 to 1.5
- w_in: bfloat16 [6144, 24576], P('gz', ('gx', 'gy')), may hold values from -0.078125 to 0.078125
- b_in: float32 [24576], P('gx'), may hold values from -4 to 4
- w_out: bfloat16 [24576, 6144], P('gx', ('gz', 'gy')), may hold values from -0.0390625 to 0.0390625
- cotangent: bfloat16 [768, 6144], P(('gy', 'gx'), 'gz'), may hold values from -6 to 6
Outputs:
- y_branch: bfloat16 [768, 6144], P(('gy', 'gx'), 'gz')
- input_grad: bfloat16 [768, 6144], P(('gy', 'gx'), 'gz')
- w_in_grad: bfloat16 [6144, 24576], P('gz', ('gx', 'gy'))
- w_out_grad: bfloat16 [24576, 6144], P('gx', ('gz', 'gy'))
- bias_grad: float32 [24576], P('gx')
- gain_grad: float32 [6144], P('gz')
All inputs are finite; a program needn't handle non-finite values.
Results may differ from a plain program's by a relative error of at most 0.02.
Values may be sent and summed in bfloat16 or wider, within the bound.
A program may use at most 64 MiB of HBM per device.

v0:
```python
import jax
import jax.numpy as jnp
from jax import lax
from jax.sharding import PartitionSpec as P

epsilon = 1e-06


def contract_last(left_side, right_side):
    return lax.dot_general(
        left_side, right_side, (((1,), (1,)), ((), ())), preferred_element_type=jnp.float32
    )


def contract_first(left_side, right_side):
    return lax.dot_general(
        left_side, right_side, (((0,), (0,)), ((), ())), preferred_element_type=jnp.float32
    )


def shards(tokens, gain, w_in, b_in, w_out, cotangent):
    floats = tokens.astype(jnp.float32)
    row_sums, row_squares = lax.psum((jnp.sum(floats, 1), jnp.sum(floats * floats, 1)), "gz")
    feature_count = floats.shape[1] * lax.axis_size("gz")
    row_mean = (row_sums / feature_count)[:, None]
    row_var = (row_squares / feature_count)[:, None] - row_mean * row_mean
    inv_std = lax.rsqrt(row_var + epsilon)
    centred = (floats - row_mean) * inv_std
    normed = (centred * gain).astype(jnp.bfloat16)
    normed_all = lax.all_gather(normed, "gx", axis=0, tiled=True)
    grad_all = lax.all_gather(cotangent, "gx", axis=0, tiled=True)
    w_in_use = lax.all_gather(w_in, "gy", axis=1, tiled=True)
    w_out_use = lax.all_gather(w_out, "gy", axis=1, tiled=True)
    pre = (
        lax.psum_scatter(
            jnp.dot(normed_all, w_in_use, preferred_element_type=jnp.float32).astype(jnp.bfloat16),
            "gz",
            scatter_dimension=0,
            tiled=True,
        ).astype(jnp.float32)
        + b_in
    )
    activated, gelu_back = jax.vjp(jax.nn.gelu, pre)
    activated = activated.astype(jnp.bfloat16)
    act_all = lax.all_gather(activated, "gz", axis=0, tiled=True)
    y_branch = lax.psum_scatter(
        jnp.dot(act_all, w_out_use, preferred_element_type=jnp.float32).astype(jnp.bfloat16),
        "gx",
        scatter_dimension=0,
        tiled=True,
    )
    act_grad = lax.psum_scatter(
        contract_last(grad_all, w_out_use).astype(jnp.bfloat16),
        "gz",
        scatter_dimension=0,
        tiled=True,
    ).astype(jnp.float32)
    pre_grad = gelu_back(act_grad)[0].astype(jnp.bfloat16)
    bias_term = jnp.sum(pre_grad.astype(jnp.float32), 0)
    bias_grad = lax.psum(bias_term, ("gy", "gz"))
    pre_grad_all = lax.all_gather(pre_grad, "gz", axis=0, tiled=True)
    w_out_grad = lax.psum_scatter(
        contract_first(act_all, grad_all).astype(jnp.bfloat16),
        "gy",
        scatter_dimension=1,
        tiled=True,
    )
    norm_grad = lax.psum_scatter(
        contract_last(pre_grad_all, w_in_use).astype(jnp.bfloat16),
        "gx",
        scatter_dimension=0,
        tiled=True,
    ).astype(jnp.float32)
    w_in_grad = lax.psum_scatter(
        contract_first(normed_all, pre_grad_all).astype(jnp.bfloat16),
        "gy",
        scatter_dimension=1,
        tiled=True,
    )
    hat_grad = norm_grad * gain
    first_sum, second_sum = lax.psum((jnp.sum(hat_grad, 1), jnp.sum(hat_grad * centred, 1)), "gz")
    first_mean = (first_sum / feature_count)[:, None]
    second_mean = (second_sum / feature_count)[:, None]
    input_grad = ((hat_grad - first_mean - centred * second_mean) * inv_std).astype(jnp.bfloat16)
    gain_grad = lax.psum(jnp.sum(norm_grad * centred, 0), ("gx", "gy"))
    return (y_branch, input_grad, w_in_grad, w_out_grad, bias_grad, gain_grad)


def solution(mesh):
    placed = (
        P(("gy", "gx"), "gz"),
        P("gz"),
        P("gz", ("gx", "gy")),
        P("gx"),
        P("gx", ("gz", "gy")),
        P(("gy", "gx"), "gz"),
    )
    return jax.shard_map(
        shards,
        mesh=mesh,
        in_specs=placed,
        out_specs=(
            P(("gy", "gx"), "gz"),
            P(("gy", "gx"), "gz"),
            P("gz", ("gx", "gy")),
            P("gx", ("gz", "gy")),
            P("gx"),
            P("gz"),
        ),
        check_vma=False,
    )
```

profile of v0, /device:TPU:1, one launch (start us, length us, event | category | flops | bytes accessed | tf_op | source)
XLA Modules:
  0.0 629.8 jit_solution(1541445874636151068)
XLA Ops:
  7.2 0.7 all-gather.9.cloned.1.call-update
  8.0 0.7 all-gather.5.cloned.1.call-update
  8.7 23.3 %all_gather.22 = bf16[192,768]{1,0:T(8,128)(2,1)S(1)} all-gather(bf16[24,768]{1,0:T(8,128)(2,1)S(1)} %copy-done.3), channel_id=1, replica_groups=mesh['gx'=8,'gy'=4,'gz'=8] {'gx'}, dimensions={0}, use_global_device_ids=true | all-gather | bytes 331776 | tf_op jit(solution)/shard_map/all_gather | solution.py:31
  32.1 35.5 %all-gather.9.cloned.1.call-done = bf16[3072,768]{0,1:T(8,128)(2,1)} async-done(((bf16[3072,192]{0,1:T(8,128)(2,1)}), bf16[3072,768]{0,1:T(8,128)(2,1)}) %all-gather.9.cloned.1.call-update) | async-done | bytes 4718608 | tf_op jit(solution)/shard_map/all_gather | solution.py:33
  67.5 4.4 convolution_convert_fusion.2
  72.0 0.0 reduce-scatter.7.cloned.1.call-start
  72.1 0.1 convert_reduce_fusion.1
  72.2 20.2 %all-reduce.1 = (f32[24]{0:T(128)S(1)}, f32[24]{0:T(128)S(1)}) all-reduce(f32[24]{0:T(128)S(1)} %get-tuple-element.10, f32[24]{0:T(128)S(1)} %get-tuple-element.9), channel_id=1, replica_groups=mesh['gx'=8,'gy'=4,'gz'=8] {'gz'}, use_global_device_ids=true, to_apply=%region_3.0 | all-reduce | flops 48 | bytes 384 | tf_op jit(solution)/shard_map/psum | solution.py:23
  92.4 0.1 fusion.23
  92.5 21.2 %all_gather.18 = bf16[192,768]{1,0:T(8,128)(2,1)S(1)} all-gather(bf16[24,768]{1,0:T(8,128)(2,1)S(1)} %fusion.23), channel_id=1, replica_groups=mesh['gx'=8,'gy'=4,'gz'=8] {'gx'}, dimensions={0}, use_global_device_ids=true | all-gather | bytes 331776 | tf_op jit(solution)/shard_map/all_gather | solution.py:30
  113.7 10.2 %all-gather.5.cloned.1.call-done = bf16[768,3072]{1,0:T(8,128)(2,1)} async-done(((bf16[768,768]{1,0:T(8,128)(2,1)}), bf16[768,3072]{1,0:T(8,128)(2,1)}) %all-gather.5.cloned.1.call-update) | async-done | bytes 4718608 | tf_op jit(solution)/shard_map/all_gather | solution.py:32
  123.9 4.4 convolution_convert_fusion.3
  128.4 0.0 all-gather.11.cloned.1.call-start
  128.5 77.1 %reduce-scatter.11.cloned.1.call-done = bf16[24,3072]{1,0:T(8,128)(2,1)} async-done(((bf16[192,3072]{1,0:T(8,128)(2,1)}), bf16[24,3072]{1,0:T(8,128)(2,1)}) %reduce-scatter.11.cloned.1.call-update) | async-done | bytes 147472 | tf_op jit(solution)/shard_map/reduce_scatter | solution.py:52
  205.5 82.5 %reduce-scatter.7.cloned.1.call-done = bf16[24,3072]{1,0:T(8,128)(2,1)} async-done(((bf16[192,3072]{1,0:T(8,128)(2,1)}), bf16[24,3072]{1,0:T(8,128)(2,1)}) %reduce-scatter.7.cloned.1.call-update) | async-done | bytes 147472 | tf_op jit(solution)/shard_map/reduce_scatter | solution.py:35
  288.0 1.9 convert_reduce_fusion
  290.0 0.5 all-gather.7.cloned.1.call-update
  290.6 53.2 %all-gather.11.cloned.1.call-done = bf16[192,3072]{1,0:T(8,128)(2,1)} async-done(((bf16[24,3072]{1,0:T(8,128)(2,1)}), bf16[192,3072]{1,0:T(8,128)(2,1)}) %all-gather.11.cloned.1.call-update) | async-done | bytes 1179664 | tf_op jit(solution)/shard_map/all_gather | solution.py:61
  343.8 5.1 convolution_convert_fusion.4
  348.9 0.0 reduce-scatter.9.cloned.1.call-start
  349.0 50.2 %all-gather.7.cloned.1.call-done = bf16[192,3072]{1,0:T(8,128)(2,1)} async-done(((bf16[24,3072]{1,0:T(8,128)(2,1)}), bf16[192,3072]{1,0:T(8,128)(2,1)}) %all-gather.7.cloned.1.call-update) | async-done | bytes 1179664 | tf_op jit(solution)/shard_map/all_gather | solution.py:45
  399.2 5.2 convolution_convert_fusion.5
  404.4 0.0 reduce-scatter.17.cloned.1.call-start
  404.4 3.6 convolution_convert_fusion
  408.0 0.0 reduce-scatter.15.cloned.1.call-start
  408.1 1.2 copy-done.1
  409.3 3.6 convolution_convert_fusion.1
  412.9 133.6 %psum.46 = f32[3072]{0:T(1024)} all-reduce(f32[3072]{0:T(1024)S(1)} %get-tuple-element.15), channel_id=1, replica_groups=mesh['gx'=8,'gy'=4,'gz'=8] {'gy','gz'}, use_global_device_ids=true, to_apply=%region_15.0 | all-reduce | flops 3072 | bytes 24576 | tf_op jit(solution)/shard_map/psum | solution.py:60
  546.5 1.0 fusion.19
  547.5 15.9 %all-reduce = (f32[24]{0:T(128)S(1)}, f32[24]{0:T(128)S(1)}) all-reduce(f32[24]{0:T(128)S(1)} %get-tuple-element.7, f32[24]{0:T(128)S(1)} %get-tuple-element.8), channel_id=1, replica_groups=mesh['gx'=8,'gy'=4,'gz'=8] {'gz'}, use_global_device_ids=true, to_apply=%region_11.0 | all-reduce | flops 48 | bytes 384 | tf_op jit(solution)/shard_map/psum | solution.py:81
  563.4 58.1 %psum.47 = f32[768]{0:T(1024)} all-reduce(f32[768]{0:T(1024)S(1)} %get-tuple-element.6), channel_id=1, replica_groups=mesh['gx'=8,'gy'=4,'gz'=8] {'gx','gy'}, use_global_device_ids=true, to_apply=%region_17.0 | all-reduce | flops 768 | bytes 6144 | tf_op jit(solution)/shard_map/psum | solution.py:85
  621.5 1.5 fusion.17
  (29 shorter events, 0.3 us)
Async XLA Ops:
  7.2 1.5 copy-start.3
  7.2 60.4 %all-gather.9.cloned.1.call-start = ((), (), s32[]{:S(2)}) async-start(), calls=%async_computation.9 | async-start | bytes 5898240 | tf_op jit(solution)/shard_map/all_gather | solution.py:33
  7.9 116.0 %all-gather.5.cloned.1.call-start = ((), (), s32[]{:S(2)}) async-start(), calls=%async_computation.6 | async-start | bytes 5898240 | tf_op jit(solution)/shard_map/all_gather | solution.py:32
  8.7 196.9 %reduce-scatter.11.cloned.1.call-start = ((), (), s32[]{:S(2)}) async-start(), calls=%async_computation.11 | async-start | bytes 1327104 | tf_op jit(solution)/shard_map/reduce_scatter | solution.py:52
  32.1 40.0 %copy-start.2 = (bf16[24,768]{1,0:T(8,128)(2,1)S(1)}, bf16[24,768]{1,0:T(8,128)(2,1)}, u32[]{:S(2)}) copy-start(bf16[24,768]{1,0:T(8,128)(2,1)} %param.6) | copy-start | bytes 110596
  32.1 60.4 %copy-start.4 = (f32[768]{0:T(1024)S(1)}, f32[768]{0:T(1024)}, u32[]{:S(2)}) copy-start(f32[768]{0:T(1024)} %param.7) | copy-start | bytes 9220
  72.0 216.0 %reduce-scatter.7.cloned.1.call-start = ((), (), s32[]{:S(2)}) async-start(), calls=%async_computation.7 | async-start | bytes 1327104 | tf_op jit(solution)/shard_map/reduce_scatter | solution.py:35
  113.7 174.3 %copy-start.5 = (f32[3072]{0:T(1024)S(1)}, f32[3072]{0:T(1024)}, u32[]{:S(2)}) copy-start(f32[3072]{0:T(1024)} %param.9) | copy-start | bytes 36868
  128.4 215.4 %all-gather.11.cloned.1.call-start = ((), (), s32[]{:S(2)}) async-start(), calls=%async_computation.12 | async-start | bytes 1327104 | tf_op jit(solution)/shard_map/all_gather | solution.py:61
  290.0 109.2 %all-gather.7.cloned.1.call-start = ((), (), s32[]{:S(2)}) async-start(), calls=%async_computation.8 | async-start | bytes 1327104 | tf_op jit(solution)/shard_map/all_gather | solution.py:45
  290.5 256.0 %reduce-scatter.13.cloned.1.call-start = ((), (), s32[]{:S(2)}) async-start(), calls=%async_computation.13 | async-start | bytes 331776 | tf_op jit(solution)/shard_map/reduce_scatter | solution.py:68
  348.9 274.0 %reduce-scatter.9.cloned.1.call-start = ((), (), s32[]{:S(2)}) async-start(), calls=%async_computation.10 | async-start | bytes 331776 | tf_op jit(solution)/shard_map/reduce_scatter | solution.py:46
  399.2 5.3 copy-start
  404.4 218.6 %reduce-scatter.17.cloned.1.call-start = ((), (), s32[]{:S(2)}) async-start(), calls=%async_computation.15 | async-start | bytes 5898240 | tf_op jit(solution)/shard_map/reduce_scatter | solution.py:62
  408.0 1.3 copy-start.1
  408.0 214.9 %reduce-scatter.15.cloned.1.call-start = ((), (), s32[]{:S(2)}) async-start(), calls=%async_computation.14 | async-start | bytes 5898240 | tf_op jit(solution)/shard_map/reduce_scatter | solution.py:74
Sparse Core Ops, SparseCore 0:
  9.8 57.6 all-gather.8
  69.3 54.5 all-gather.4
  128.5 76.9 reduce-scatter.10
  210.5 77.4 reduce-scatter.6
  291.0 52.7 all-gather.10
  346.8 52.2 all-gather.6
  401.7 32.5 reduce-scatter.12
  437.5 35.3 reduce-scatter.8
  476.0 57.7 reduce-scatter.16
  536.8 54.4 reduce-scatter.14
where the time goes:
time: 630 us
  waiting for transfers between devices  311 us (49%)
  blocking collectives  272 us (43%)
  matrix products  26.4 us (4%)
  between operations  14.2 us (2%)
    psum x1, blocking collectives, shards(): bias_grad = lax.psum(bias_term, ('gy', 'gz'))  134 us
    reduce_scatter x1, waiting for transfers between devices, shards(): lax.psum_scatter(jnp.dot(normed_all, w_in_use, preferred_element_type=jnp...  82.5 us
    reduce_scatter x1, waiting for transfers between devices, shards(): lax.psum_scatter(contract_last(grad_all, w_out_use).astype(jnp.bfloat16),...  77.1 us
    psum x1, blocking collectives, shards(): gain_grad = lax.psum(jnp.sum(norm_grad * centred, 0), ('gx', 'gy'))  58.1 us
    all_gather x1, waiting for transfers between devices, shards(): pre_grad_all = lax.all_gather(pre_grad, 'gz', axis=0, tiled=True)  53.2 us
    all_gather x1, waiting for transfers between devices, shards(): act_all = lax.all_gather(activated, 'gz', axis=0, tiled=True)  50.2 us
    all_gather x1, waiting for transfers between devices, shards(): w_out_use = lax.all_gather(w_out, 'gy', axis=1, tiled=True)  35.5 us
    all_gather x1, blocking collectives, shards(): grad_all = lax.all_gather(cotangent, 'gx', axis=0, tiled=True)  23.3 us
  transfers between devices with their start and end apart: 10, of which 6 were waited for; matrix products, arithmetic and copies ran while one was open for 5% of the time, Pallas kernels for 0%

commit v1 on v0

--- a/solution.py
+++ b/solution.py
@@ -27,28 +27,23 @@
     inv_std = lax.rsqrt(row_var + epsilon)
     centred = (floats - row_mean) * inv_std
     normed = (centred * gain).astype(jnp.bfloat16)
-    normed_all = lax.all_gather(normed, "gx", axis=0, tiled=True)
-    grad_all = lax.all_gather(cotangent, "gx", axis=0, tiled=True)
-    w_in_use = lax.all_gather(w_in, "gy", axis=1, tiled=True)
-    w_out_use = lax.all_gather(w_out, "gy", axis=1, tiled=True)
+    normed_all = lax.all_gather(normed, ("gy", "gx"), axis=0, tiled=True)
+    grad_all = lax.all_gather(cotangent, ("gy", "gx"), axis=0, tiled=True)
+    w_out_use = lax.all_to_all(w_out, "gy", split_axis=0, concat_axis=1, tiled=True)
+    hidden = w_in.shape[1]
+    bias = lax.dynamic_slice_in_dim(b_in, lax.axis_index("gy") * hidden, hidden)
     pre = (
         lax.psum_scatter(
-            jnp.dot(normed_all, w_in_use, preferred_element_type=jnp.float32).astype(jnp.bfloat16),
+            jnp.dot(normed_all, w_in, preferred_element_type=jnp.float32).astype(jnp.bfloat16),
             "gz",
             scatter_dimension=0,
             tiled=True,
         ).astype(jnp.float32)
-        + b_in
+        + bias
     )
     activated, gelu_back = jax.vjp(jax.nn.gelu, pre)
     activated = activated.astype(jnp.bfloat16)
     act_all = lax.all_gather(activated, "gz", axis=0, tiled=True)
-    y_branch = lax.psum_scatter(
-        jnp.dot(act_all, w_out_use, preferred_element_type=jnp.float32).astype(jnp.bfloat16),
-        "gx",
-        scatter_dimension=0,
-        tiled=True,
-    )
     act_grad = lax.psum_scatter(
         contract_last(grad_all, w_out_use).astype(jnp.bfloat16),
         "gz",
@@ -56,27 +51,29 @@
         tiled=True,
     ).astype(jnp.float32)
     pre_grad = gelu_back(act_grad)[0].astype(jnp.bfloat16)
-    bias_term = jnp.sum(pre_grad.astype(jnp.float32), 0)
-    bias_grad = lax.psum(bias_term, ("gy", "gz"))
     pre_grad_all = lax.all_gather(pre_grad, "gz", axis=0, tiled=True)
-    w_out_grad = lax.psum_scatter(
+    w_out_grad = lax.all_to_all(
         contract_first(act_all, grad_all).astype(jnp.bfloat16),
         "gy",
-        scatter_dimension=1,
+        split_axis=1,
+        concat_axis=0,
+        tiled=True,
+    )
+    y_branch = lax.psum_scatter(
+        jnp.dot(act_all, w_out_use, preferred_element_type=jnp.float32).astype(jnp.bfloat16),
+        ("gy", "gx"),
+        scatter_dimension=0,
         tiled=True,
     )
     norm_grad = lax.psum_scatter(
-        contract_last(pre_grad_all, w_in_use).astype(jnp.bfloat16),
-        "gx",
+        contract_last(pre_grad_all, w_in).astype(jnp.bfloat16),
+        ("gy", "gx"),
         scatter_dimension=0,
         tiled=True,
     ).astype(jnp.float32)
-    w_in_grad = lax.psum_scatter(
-        contract_first(normed_all, pre_grad_all).astype(jnp.bfloat16),
-        "gy",
-        scatter_dimension=1,
-        tiled=True,
-    )
+    w_in_grad = contract_first(normed_all, pre_grad_all).astype(jnp.bfloat16)
+    bias_term = jnp.sum(pre_grad_all.astype(jnp.float32), 0)
+    bias_grad = lax.all_gather(bias_term, "gy", axis=0, tiled=True)
     hat_grad = norm_grad * gain
     first_sum, second_sum = lax.psum((jnp.sum(hat_grad, 1), jnp.sum(hat_grad * centred, 1)), "gz")
     first_mean = (first_sum / feature_count)[:, None]

time: 630 us -> 738 us (1.17)
  waiting for transfers between devices: 311 us -> 543 us
  blocking collectives: 272 us -> 142 us
  matrix products: 26.4 us -> 17.9 us
    psum x1 -> x0, blocking collectives: 134 us -> none  [shards(): bias_grad = lax.psum(bias_term, ('gy', 'gz'))]
    all_gather x2, waiting for transfers between devices: 45.7 us -> 152 us  [the longest x1 99.7 us: shards(): normed_all = lax.all_gather(normed, ('gy', 'gx'), axis=0, tiled=True)]
    reduce_scatter x4 -> x2, waiting for transfers between devices: 82.5 us -> 167 us  [the longest x1 84.2 us: shards(): lax.psum_scatter(contract_last(pre_grad_all, w_in).astype(jnp.bfloat16),...]
    reduce_scatter x1, waiting for transfers between devices: 0.01 us -> 35.8 us  [shards(): lax.psum_scatter(jnp.dot(act_all, w_out_use, preferred_element_type=jnp.f...]
    all_gather x2 -> x1, blocking collectives: 44.5 us -> 17.2 us  [shards(): bias_grad = lax.all_gather(bias_term, 'gy', axis=0, tiled=True)]
    all_to_all x0 -> x1, blocking collectives: none -> 23.2 us  [shards(): lax.all_to_all(w_out, 'gy', split_axis=0, concat_axis=1, tiled=True)]
  transfers between devices with their start and end apart: 10 -> 9, of which waited for: 6 -> 8; matrix products, arithmetic and copies ran while one was open for 5% -> 4% of each run, Pallas kernels for 0% -> 0%
where the time goes in v1:
time: 738 us; the launch traced here: 736 us
  waiting for transfers between devices  543 us (74%)
  blocking collectives  142 us (19%)
  matrix products  17.9 us (2%)
  between operations  14.2 us (2%)
    all_gather x1, waiting for transfers between devices, shards(): normed_all = lax.all_gather(normed, ('gy', 'gx'), axis=0, tiled=True)  99.7 us
    reduce_scatter x1, waiting for transfers between devices, shards(): lax.psum_scatter(contract_last(pre_grad_all, w_in).astype(jnp.bfloat16),...  84.2 us
    reduce_scatter x1, waiting for transfers between devices, shards(): lax.psum_scatter(jnp.dot(normed_all, w_in, preferred_element_type=jnp.flo...  82.5 us
    reduce_scatter x1, waiting for transfers between devices, shards(): lax.psum_scatter(contract_last(grad_all, w_out_use).astype(jnp.bfloat16),...  81.4 us
    psum x1, blocking collectives, shards(): gain_grad = lax.psum(jnp.sum(norm_grad * centred, 0), ('gx', 'gy'))  59.7 us
    all_gather x1, waiting for transfers between devices, shards(): pre_grad_all = lax.all_gather(pre_grad, 'gz', axis=0, tiled=True)  53.3 us
    all_gather x1, waiting for transfers between devices, shards(): grad_all = lax.all_gather(cotangent, ('gy', 'gx'), axis=0, tiled=True)  52.7 us
    all_gather x1, waiting for transfers between devices, shards(): act_all = lax.all_gather(activated, 'gz', axis=0, tiled=True)  51.9 us
  transfers between devices with their start and end apart: 9, of which 8 were waited for; matrix products, arithmetic and copies ran while one was open for 4% of the time, Pallas kernels for 0%

profile of v1, /device:TPU:1, one launch (start us, length us, event | category | flops | bytes accessed | tf_op | source)
XLA Modules:
  0.0 735.6 jit_solution(11449686170635625742)
XLA Ops:
  7.2 0.7 all-gather.10.cloned.1.call-update
  8.0 0.9 convert_reduce_fusion.1
  8.8 21.4 %all-reduce.1 = (f32[24]{0:T(128)S(1)}, f32[24]{0:T(128)S(1)}) all-reduce(f32[24]{0:T(128)S(1)} %get-tuple-element.10, f32[24]{0:T(128)S(1)} %get-tuple-element.9), channel_id=1, replica_groups=mesh['gx'=8,'gy'=4,'gz'=8] {'gz'}, use_global_device_ids=true, to_apply=%region_3.0 | all-reduce | flops 48 | bytes 384 | tf_op jit(solution)/shard_map/psum | solution.py:23
  30.8 1.5 fusion.23
  32.3 1.4 copy.21
  33.7 23.2 %all_to_all.38 = bf16[4,768,192]{1,2,0:T(8,128)(2,1)S(1)} all-to-all(bf16[4,768,192]{1,2,0:T(8,128)(2,1)S(1)} %bitcast.25), channel_id=1, replica_groups=mesh['gx'=8,'gy'=4,'gz'=8] {'gy'}, dimensions={0} | all-to-all | bytes 2359296 | tf_op jit(solution)/shard_map/all_to_all | solution.py:32
  56.8 52.7 %all-gather.10.cloned.1.call-done = bf16[768,768]{1,0:T(8,128)(2,1)} async-done(((bf16[24,768]{1,0:T(8,128)(2,1)}), bf16[768,768]{1,0:T(8,128)(2,1)}) %all-gather.10.cloned.1.call-update) | async-done | bytes 1179664 | tf_op jit(solution)/shard_map/all_gather | solution.py:31
  109.5 3.4 convolution_convert_fusion.3
  112.9 99.7 %all-gather.6.cloned.1.call-done = bf16[768,768]{1,0:T(8,128)(2,1)} async-done(((bf16[24,768]{1,0:T(8,128)(2,1)}), bf16[768,768]{1,0:T(8,128)(2,1)}) %all-gather.6.cloned.1.call-update) | async-done | bytes 1179664 | tf_op jit(solution)/shard_map/all_gather | solution.py:30
  212.6 3.4 convolution_convert_fusion.5
  216.1 0.8 dynamic_slice.3
  216.8 81.4 %reduce-scatter.9.cloned.1.call-done = bf16[96,768]{1,0:T(8,128)(2,1)} async-done(((bf16[768,768]{1,0:T(8,128)(2,1)}), bf16[96,768]{1,0:T(8,128)(2,1)}) %reduce-scatter.9.cloned.1.call-update) | async-done | bytes 147472 | tf_op jit(solution)/shard_map/reduce_scatter | solution.py:47
  298.2 82.5 %reduce-scatter.5.cloned.1.call-done = bf16[96,768]{1,0:T(8,128)(2,1)} async-done(((bf16[768,768]{1,0:T(8,128)(2,1)}), bf16[96,768]{1,0:T(8,128)(2,1)}) %reduce-scatter.5.cloned.1.call-update) | async-done | bytes 147472 | tf_op jit(solution)/shard_map/reduce_scatter | solution.py:36
  380.7 1.9 fusion.2
  382.7 0.5 all-gather.8.cloned.1.call-update
  383.3 53.3 %all-gather.12.cloned.1.call-done = bf16[768,768]{1,0:T(8,128)(2,1)} async-done(((bf16[96,768]{1,0:T(8,128)(2,1)}), bf16[768,768]{1,0:T(8,128)(2,1)}) %all-gather.12.cloned.1.call-update) | async-done | bytes 1179664 | tf_op jit(solution)/shard_map/all_gather | solution.py:54
  436.5 3.4 convolution_convert_fusion.2
  440.1 51.9 %all-gather.8.cloned.1.call-done = bf16[768,768]{1,0:T(8,128)(2,1)} async-done(((bf16[96,768]{1,0:T(8,128)(2,1)}), bf16[768,768]{1,0:T(8,128)(2,1)}) %all-gather.8.cloned.1.call-update) | async-done | bytes 1179664 | tf_op jit(solution)/shard_map/all_gather | solution.py:46
  491.9 3.5 convolution_convert_fusion.4
  495.5 1.2 copy-done.6
  496.7 2.1 convolution_convert_fusion
  498.8 5.9 all-to-all-start.1
  504.9 17.2 %all-gather = f32[4,1,768]{2,1,0:T(1,128)S(1)} all-gather(f32[1,1,768]{2,1,0:T(1,128)S(1)} %reshape.28), channel_id=1, replica_groups=mesh['gx'=8,'gy'=4,'gz'=8] {'gy'}, dimensions={0}, use_global_device_ids=true | all-gather | bytes 15360 | tf_op jit(solution)/shard_map/all_gather | solution.py:76
  522.2 2.1 convolution_convert_fusion.1
  524.3 1.2 copy.19
  525.5 84.2 %reduce-scatter.11.cloned.1.call-done = bf16[24,768]{1,0:T(8,128)(2,1)} async-done(((bf16[768,768]{1,0:T(8,128)(2,1)}), bf16[24,768]{1,0:T(8,128)(2,1)}) %reduce-scatter.11.cloned.1.call-update) | async-done | bytes 36880 | tf_op jit(solution)/shard_map/reduce_scatter | solution.py:68
  609.7 1.0 fusion.19
  610.7 20.6 %all-reduce = (f32[24]{0:T(128)S(1)}, f32[24]{0:T(128)S(1)}) all-reduce(f32[24]{0:T(128)S(1)} %get-tuple-element.7, f32[24]{0:T(128)S(1)} %get-tuple-element.8), channel_id=1, replica_groups=mesh['gx'=8,'gy'=4,'gz'=8] {'gz'}, use_global_device_ids=true, to_apply=%region_11.0 | all-reduce | flops 48 | bytes 384 | tf_op jit(solution)/shard_map/psum | solution.py:78
  631.2 59.7 %psum.39 = f32[768]{0:T(1024)} all-reduce(f32[768]{0:T(1024)S(1)} %get-tuple-element.6), channel_id=1, replica_groups=mesh['gx'=8,'gy'=4,'gz'=8] {'gx','gy'}, use_global_device_ids=true, to_apply=%region_14.0 | all-reduce | flops 768 | bytes 6144 | tf_op jit(solution)/shard_map/psum | solution.py:82
  690.9 1.5 fusion.17
  692.4 35.8 %reduce-scatter.7.cloned.1.call-done = bf16[24,768]{1,0:T(8,128)(2,1)} async-done(((bf16[768,768]{1,0:T(8,128)(2,1)}), bf16[24,768]{1,0:T(8,128)(2,1)}) %reduce-scatter.7.cloned.1.call-update) | async-done | bytes 36880 | tf_op jit(solution)/shard_map/reduce_scatter | solution.py:62
  728.2 0.6 copy.23
  (36 shorter events, 1.2 us)
Async XLA Ops:
  7.2 205.4 %copy-start = (bf16[768,768]{1,0:T(8,128)(2,1)S(1)}, bf16[768,768]{1,0:T(8,128)(2,1)}, u32[]{:S(2)}) copy-start(bf16[768,768]{1,0:T(8,128)(2,1)} %param.8) | copy-start | bytes 3538948
  7.2 102.3 %all-gather.10.cloned.1.call-start = ((), (), s32[]{:S(2)}) async-start(), calls=%async_computation.10 | async-start | bytes 1216512 | tf_op jit(solution)/shard_map/all_gather | solution.py:31
  7.9 204.7 %all-gather.6.cloned.1.call-start = ((), (), s32[]{:S(2)}) async-start(), calls=%async_computation.6 | async-start | bytes 1216512 | tf_op jit(solution)/shard_map/all_gather | solution.py:30
  30.3 0.5 copy-start.4
  32.3 265.9 %reduce-scatter.9.cloned.1.call-start = ((), (), s32[]{:S(2)}) async-start(), calls=%async_computation.11 | async-start | bytes 1327104 | tf_op jit(solution)/shard_map/reduce_scatter | solution.py:47
  112.9 267.8 %reduce-scatter.5.cloned.1.call-start = ((), (), s32[]{:S(2)}) async-start(), calls=%async_computation.7 | async-start | bytes 1327104 | tf_op jit(solution)/shard_map/reduce_scatter | solution.py:36
  216.0 220.5 %all-gather.12.cloned.1.call-start = ((), (), s32[]{:S(2)}) async-start(), calls=%async_computation.12 | async-start | bytes 1327104 | tf_op jit(solution)/shard_map/all_gather | solution.py:54
  382.6 109.3 %all-gather.8.cloned.1.call-start = ((), (), s32[]{:S(2)}) async-start(), calls=%async_computation.8 | async-start | bytes 1327104 | tf_op jit(solution)/shard_map/all_gather | solution.py:46
  383.2 226.5 %reduce-scatter.11.cloned.1.call-start = ((), (), s32[]{:S(2)}) async-start(), calls=%async_computation.13 | async-start | bytes 1216512 | tf_op jit(solution)/shard_map/reduce_scatter | solution.py:68
  440.0 288.2 %reduce-scatter.7.cloned.1.call-start = ((), (), s32[]{:S(2)}) async-start(), calls=%async_computation.9 | async-start | bytes 1216512 | tf_op jit(solution)/shard_map/reduce_scatter | solution.py:62
  491.9 3.5 copy-start.8
  495.4 1.3 copy-start.6
  498.8 5.9 copy-start.1
  498.8 25.5 %all-to-all-start.1 = ((bf16[768,4,192]{0,2,1:T(8,128)(2,1)}), bf16[768,4,192]{0,2,1:T(8,128)(2,1)S(1)}, u32[]{:S(2)}, u32[]{:S(2)}) async-start(bf16[768,4,192]{0,2,1:T(8,128)(2,1)} %bitcast.30), calls=%async_computation.5 | async-start | bytes 2359296 | tf_op jit(solution)/shard_map/all_to_all | solution.py:55
  504.7 17.5 %copy-start.7 = (bf16[768,768]{1,0:T(8,128)(2,1)S(1)}, bf16[768,768]{1,0:T(8,128)(2,1)}, u32[]{:S(2)}) copy-start(bf16[768,768]{1,0:T(8,128)(2,1)} %all-gather.6.cloned.1.call-done) | copy-start | bytes 3538948
  524.3 85.4 %copy-start.2 = (bf16[24,768]{1,0:T(8,128)(2,1)S(1)}, bf16[24,768]{1,0:T(8,128)(2,1)}, u32[]{:S(2)}) copy-start(bf16[24,768]{1,0:T(8,128)(2,1)} %param.6) | copy-start | bytes 110596
  524.3 85.4 %copy-start.3 = (f32[768]{0:T(1024)S(1)}, f32[768]{0:T(1024)}, u32[]{:S(2)}) copy-start(f32[768]{0:T(1024)} %param.7) | copy-start | bytes 9220
  524.3 85.4 %copy-start.5 = (f32[24]{0:T(128)S(1)}, f32[24]{0:T(128)}, u32[]{:S(2)}) copy-start(f32[24]{0:T(128)} %copy-done.4) | copy-start | bytes 292
Sparse Core Ops, SparseCore 0:
  9.8 99.6 all-gather.9
  111.9 100.6 all-gather.5
  217.2 80.9 reduce-scatter.8
  303.2 77.4 reduce-scatter.4
  383.7 52.7 all-gather.11
  439.6 52.2 all-gather.7
  494.4 115.2 reduce-scatter.10
  612.9 115.2 reduce-scatter.6

commit v2 on v1

v2 whole, which is shorter than its diff:
```python
import functools

import jax
import jax.numpy as jnp
from jax import lax
from jax.experimental import pallas as pl
from jax.experimental.pallas import tpu as pltpu
from jax.sharding import PartitionSpec as P

epsilon = 1e-06
MESH = pl.DeviceIdType.MESH
BF = jnp.bfloat16
F32 = jnp.float32
NZ = 8
NX = 4
W = 768
CH = 192
HALF = CH // 2
SH = 24
FB = 192
TILE = 256
LANES = 128
COPIES = 140
FEATURES = W * NZ
ROOT = 0.7978845608028654
CUBIC = 0.044715


class Net:
    def __init__(self, send_sems, recv_sems):
        self.send_sems, self.recv_sems = send_sems, recv_sems
        self.count = 0
        self.sent = []

    def send(self, src, dst, **where):
        copy = pltpu.make_async_remote_copy(
            src_ref=src,
            dst_ref=dst,
            send_sem=self.send_sems.at[self.count],
            recv_sem=self.recv_sems.at[self.count],
            device_id=where,
            device_id_type=MESH,
        )
        self.count += 1
        copy.start()
        self.sent.append(copy)
        return copy

    def drain(self):
        for copy in self.sent:
            copy.wait_send()


def dot(left, right, left_dim, right_dim):
    return lax.dot_general(
        left, right, (((left_dim,), (right_dim,)), ((), ())), preferred_element_type=F32
    )


def rows_of(chunk):
    return pl.ds(pl.multiple_of(chunk * CH, CH), CH)


def tiles(body, count=W // TILE, size=TILE):
    def step(i, carry):
        body(pl.ds(pl.multiple_of(i * size, size), size))
        return carry

    lax.fori_loop(0, count, step, 0)


def kernel(
    tok, gain, w_in, b_in, w_out, cot,
    y_out, in_grad, w_in_grad, w_out_grad, b_grad, g_grad,
    g_cot, g_nor, cot_all, nor_all, act_all, pg_all, w_blk, w_full, w_send,
    stat_in, far, side_f, side_b, own, relay, inbox, yx_out, yx_in, pre,
    keep, core_out, core_in, z_out, z_in, total, ty_out, ty_in,
    stat2_in, gz_in, gy_in,
    send_sems, recv_sems,
):
    z, g, q = lax.axis_index("gx"), lax.axis_index("gy"), lax.axis_index("gz")
    yl, c = lax.div(g, 2), lax.rem(g, 2)
    x, h = lax.div(q, 2), lax.rem(q, 2)
    net = Net(send_sems, recv_sems)

    def ring(value, step, size):
        return lax.rem(value + (step + size), size)

    def z_at(step):
        return ring(z, step, NZ)

    def q_at(step):
        return ring(q, step, NZ)

    def g_at(step):
        return ring(g, step, 4)

    def x_at(step):
        return ring(x, step, NX)

    def x_dev(step):
        return x_at(step) * 2 + h

    y_peer = (1 - yl) * 2 + c
    core_peer = yl * 2 + (1 - c)
    h_peer = x * 2 + (1 - h)

    barrier = pltpu.get_barrier_semaphore()
    for s in range(1, NZ):
        pl.semaphore_signal(barrier, inc=1, device_id={"gx": z_at(s)}, device_id_type=MESH)
        pl.semaphore_signal(barrier, inc=1, device_id={"gz": q_at(s)}, device_id_type=MESH)
    for s in range(1, 4):
        pl.semaphore_signal(barrier, inc=1, device_id={"gy": g_at(s)}, device_id_type=MESH)
    pl.semaphore_wait(barrier, 2 * (NZ - 1) + 3)

    turned = [
        net.send(
            w_out.at[pl.ds(pl.multiple_of(g_at(s) * W, W), W)], w_blk.at[g], gy=g_at(s)
        )
        for s in range(1, 4)
    ]
    g_cot[c, z, yl] = cot[...]
    cot_y = net.send(g_cot.at[c, z, yl], g_cot.at[c, z, yl], gy=y_peer)

    lane = lax.broadcasted_iota(jnp.int32, (SH, LANES), 1)

    def pair_tile(first, second):
        return jnp.where(lane < LANES // 2, first, second)

    def split_pair(both):
        return both[:, 0:1], both[:, LANES // 2 : LANES // 2 + 1]

    floats = tok[...].astype(F32)
    stat_in[0] = pair_tile(
        jnp.sum(floats, 1, keepdims=True), jnp.sum(floats * floats, 1, keepdims=True)
    )
    stats = [net.send(stat_in.at[0], stat_in.at[s], gz=q_at(s)) for s in range(1, NZ)]

    class Gather:
        def __init__(self, buf, first):
            self.buf, self.first = buf, first
            self.right, self.left, self.cores = {}, {}, []

        def block(self, step):
            return self.buf.at[c, z_at(step)]

        def forward(self, step, right, left):
            block = self.block(step)
            if right:
                self.right[1 - step] = net.send(block, block, gx=z_at(1))
            if left:
                self.left[1 + step] = net.send(block, block, gx=z_at(-1))
            self.cores.append(net.send(block, block, gy=core_peer))

        def begin(self):
            self.first.wait_recv()
            self.forward(0, True, True)

        def from_left(self, n):
            self.right[n].wait_recv()
            self.forward(-n, n < 4, False)

        def from_right(self, n):
            self.left[n].wait_recv()
            self.forward(n, False, n < 3)

        def finish(self, whole):
            for copy in self.cores:
                copy.wait_recv()
            for block in range(4):
                piece = self.buf[block % 2, :, block // 2].astype(F32).reshape(CH, W)
                whole[pl.ds(block * CH, CH), :] = piece.astype(BF)

    cots = Gather(g_cot, cot_y)
    cots.begin()

    for copy in stats:
        copy.wait_recv()
    both = stat_in[0]
    for s in range(1, NZ):
        both = both + stat_in[s]
    row_sum, row_square = split_pair(both)
    row_mean = row_sum / FEATURES
    row_var = row_square / FEATURES - row_mean * row_mean
    inv_std = lax.rsqrt(row_var + epsilon)

    def centre():
        return (tok[...].astype(F32) - row_mean) * inv_std

    g_nor[c, z, yl] = (centre() * gain[...]).astype(BF)
    nors = Gather(g_nor, net.send(g_nor.at[c, z, yl], g_nor.at[c, z, yl], gy=y_peer))

    cots.from_left(1)
    cots.from_right(1)
    nors.begin()
    cots.from_left(2)
    cots.from_right(2)
    nors.from_left(1)
    nors.from_right(1)
    cots.from_left(3)
    cots.from_right(3)
    nors.from_left(2)
    nors.from_right(2)
    cots.from_left(4)
    nors.from_left(3)
    nors.from_right(3)
    nors.from_left(4)
    nors.finish(nor_all)

    class HiddenSum:
        def __init__(self, n, product):
            self.n, self.product = n, product

        def begin(self):
            n = self.n

            def far_tile(cols):
                far[n, :, cols] = self.product(x_at(2), cols).astype(BF)

            tiles(far_tile)
            self.relays = [
                net.send(far.at[n, pl.ds(0, HALF)], relay.at[n, 0], gz=x_dev(1)),
                net.send(far.at[n, pl.ds(HALF, HALF)], relay.at[n, 1], gz=x_dev(-1)),
            ]
            self.raw = []
            for side, step in enumerate((1, -1)):

                def side_tile(cols):
                    value = self.product(x_at(step), cols)
                    side_f[n, side, :, cols] = value[side * HALF : (side + 1) * HALF]
                    other = 1 - side
                    side_b[n, side, pl.ds(other * HALF, HALF), cols] = value[
                        other * HALF : (other + 1) * HALF
                    ].astype(BF)

                tiles(side_tile)
                part = pl.ds((1 - side) * HALF, HALF)
                self.raw.append(
                    net.send(side_b.at[n, side, part], inbox.at[n, side, part], gz=x_dev(step))
                )

            def own_tile(cols):
                own[n, :, cols] = self.product(x, cols)

            tiles(own_tile)

        def relayed(self):
            n = self.n
            self.summed = []
            for side, step in enumerate((1, -1)):
                self.relays[side].wait_recv()
                part = pl.ds(side * HALF, HALF)

                def add_tile(cols):
                    value = side_f[n, side, :, cols] + relay[n, side, :, cols].astype(F32)
                    side_b[n, side, part, cols] = value.astype(BF)

                tiles(add_tile)
                self.summed.append(
                    net.send(side_b.at[n, side, part], inbox.at[n, side, part], gz=x_dev(step))
                )

        def pair_up(self):
            n = self.n
            self.pairs = []
            for part_index in range(2):
                part = pl.ds(part_index * HALF, HALF)
                self.summed[part_index].wait_recv()
                self.raw[1 - part_index].wait_recv()

                def add_tile(cols):
                    value = own[n, part, cols] + inbox[n, 0, part, cols].astype(F32)
                    value = value + inbox[n, 1, part, cols].astype(F32)
                    yx_out[n, part, cols] = value.astype(BF)

                tiles(add_tile)
                self.pairs.append(
                    net.send(yx_out.at[n, part], yx_in.at[n, part], gz=h_peer)
                )

        def total(self, rows):
            n = self.n
            return yx_out[n, rows, :].astype(F32) + yx_in[n, rows, :].astype(F32)

    pres = HiddenSum(0, lambda k, cols: dot(nor_all[rows_of(k), :], w_in[:, cols], 1, 0))
    grads = HiddenSum(1, lambda k, cols: dot(cot_all[rows_of(k), :], w_full[cols, :], 1, 1))

    pres.begin()

    cots.finish(cot_all)
    w_blk[g] = w_out[pl.ds(pl.multiple_of(g * W, W), W), :]
    for copy in turned:
        copy.wait_recv()

    def assemble(rows):
        w_full[rows, :] = jnp.concatenate([w_blk[i, rows, :] for i in range(4)], axis=1)

    tiles(assemble)

    pres.relayed()
    grads.begin()
    pres.pair_up()
    grads.relayed()

    bias = b_in[:, pl.ds(pl.multiple_of(g * W, W), W)]
    mine = pl.multiple_of(x * CH, CH)

    class HiddenGather:
        def __init__(self, whole):
            self.whole = whole
            rows = whole.at[pl.ds(mine, CH)]
            self.sides = [net.send(rows, rows, gz=x_dev(step)) for step in (1, -1)]

        def onward(self):
            self.onwards = []
            for side, step in enumerate((1, -1)):
                self.sides[side].wait_recv()
                start = pl.multiple_of(x_at(-step) * CH + side * HALF, HALF)
                rows = self.whole.at[pl.ds(start, HALF)]
                self.onwards.append(net.send(rows, rows, gz=x_dev(step)))

        def finish(self):
            for copy in self.onwards:
                copy.wait_recv()

    STEP = 32
    for part_index in range(2):
        pres.pairs[part_index].wait_recv()

        def activate(i, carry):
            start = pl.multiple_of(part_index * HALF + i * STEP, STEP)
            rows = pl.ds(start, STEP)
            v = pres.total(rows) + bias
            t = jnp.tanh(ROOT * (v + CUBIC * v * v * v))
            act_all[pl.ds(pl.multiple_of(mine + start, STEP), STEP), :] = (
                0.5 * v * (1.0 + t)
            ).astype(BF)
            pre[rows, :] = 0.5 * (1.0 + t) + 0.5 * v * (1.0 - t * t) * ROOT * (
                1.0 + 3.0 * CUBIC * v * v
            )
            return carry

        lax.fori_loop(0, HALF // STEP, activate, 0)
    acts = HiddenGather(act_all)

    grads.pair_up()
    acts.onward()
    for part_index in range(2):
        grads.pairs[part_index].wait_recv()

        def backward(i, carry):
            start = pl.multiple_of(part_index * HALF + i * STEP, STEP)
            rows = pl.ds(start, STEP)
            pg_all[pl.ds(pl.multiple_of(mine + start, STEP), STEP), :] = (
                grads.total(rows) * pre[rows, :]
            ).astype(BF)
            return carry

        lax.fori_loop(0, HALF // STEP, backward, 0)
    pgs = HiddenGather(pg_all)

    class FeatureSum:
        def __init__(self, n, product):
            self.n, self.product = n, product
            self.cores, self.spread = {}, {}

        def products(self, order):
            n = self.n
            j = lax.div(x, 2) if order == 0 else 1 - lax.div(x, 2)

            def send_tile(cols):
                value = self.product(2 * j + (1 - c), cols)
                core_out[n, order, :, :, cols] = value.reshape(NZ, SH, TILE).astype(BF)

            tiles(send_tile)
            self.cores[order] = net.send(
                core_out.at[n, order], core_in.at[n, order], gy=core_peer
            )

            def keep_tile(cols):
                value = self.product(2 * j + c, cols)
                keep[n, order, :, :, cols] = value.reshape(NZ, SH, TILE)

            tiles(keep_tile)

        def scatter(self, order):
            n = self.n
            self.cores[order].wait_recv()

            def add_one(i, carry):
                value = keep[n, order, i] + core_in[n, order, i].astype(F32)
                keep[n, order, i] = value
                z_out[n, order, i] = value.astype(BF)
                return carry

            lax.fori_loop(0, NZ, add_one, 0)
            self.spread[order] = [
                net.send(z_out.at[n, order, z_at(s)], z_in.at[n, order, s - 1], gx=z_at(s))
                for s in range(1, NZ)
            ]

        def collect(self, order):
            n = self.n
            for copy in self.spread[order]:
                copy.wait_recv()
            value = keep[n, order, z]
            for s in range(NZ - 1):
                value = value + z_in[n, order, s].astype(F32)
            total[n, order] = value

        def exchange(self):
            n = self.n
            here = lax.rem(lax.div(x, 2) + yl, 2)
            ty_out[n] = total[n, 1 - here].astype(BF)
            self.last = net.send(ty_out.at[n], ty_in.at[n], gy=y_peer)
            self.here = here

        def result(self):
            self.last.wait_recv()
            return total[self.n, self.here] + ty_in[self.n].astype(F32)

    ys = FeatureSum(0, lambda k, cols: dot(act_all[rows_of(k), :], w_full[:, cols], 1, 0))
    norms = FeatureSum(1, lambda k, cols: dot(pg_all[rows_of(k), :], w_in[cols, :], 1, 1))

    ys.products(0)
    ys.scatter(0)
    acts.finish()
    ys.products(1)
    ys.scatter(1)

    def w_out_tile(rows):
        value = dot(act_all[:, rows], cot_all[...], 0, 0)
        for i in range(4):
            w_send[i, rows, :] = value[:, i * FB : (i + 1) * FB].astype(BF)

    tiles(w_out_tile)
    own_rows = pl.ds(pl.multiple_of(g * W, W), W)
    returned = [
        net.send(w_send.at[g_at(s)], w_out_grad.at[own_rows], gy=g_at(s)) for s in range(1, 4)
    ]
    w_out_grad[own_rows, :] = w_send[g]

    pgs.onward()
    ys.collect(0)
    norms.products(0)
    norms.scatter(0)
    ys.collect(1)
    ys.exchange()
    pgs.finish()
    norms.products(1)
    norms.scatter(1)

    def bias_sum(i, carry):
        rows = pl.ds(pl.multiple_of(i * STEP, STEP), STEP)
        return carry + jnp.sum(pg_all[rows, :].astype(F32), 0, keepdims=True)

    b_grad[g] = lax.fori_loop(0, W // STEP, bias_sum, jnp.zeros((1, W), F32))
    biases = [net.send(b_grad.at[g], b_grad.at[g], gy=g_at(s)) for s in range(1, 4)]

    def w_in_tile(rows):
        w_in_grad[rows, :] = dot(nor_all[:, rows], pg_all[...], 0, 0).astype(BF)

    tiles(w_in_tile)

    norms.collect(0)
    norms.collect(1)
    norms.exchange()
    y_out[...] = ys.result().astype(BF)

    norm_grad = norms.result()
    centred = centre()
    hat_grad = norm_grad * gain[...]
    stat2_in[0] = pair_tile(
        jnp.sum(hat_grad, 1, keepdims=True), jnp.sum(hat_grad * centred, 1, keepdims=True)
    )
    stats2 = [net.send(stat2_in.at[0], stat2_in.at[s], gz=q_at(s)) for s in range(1, NZ)]
    gz_in[z] = jnp.sum(norm_grad * centred, 0, keepdims=True)
    gains = [net.send(gz_in.at[z], gz_in.at[z], gx=z_at(s)) for s in range(1, NZ)]
    for copy in gains:
        copy.wait_recv()
    value = gz_in[0]
    for i in range(1, NZ):
        value = value + gz_in[i]
    gy_in[g] = value
    gains = [net.send(gy_in.at[g], gy_in.at[g], gy=g_at(s)) for s in range(1, 4)]
    for copy in stats2:
        copy.wait_recv()
    both = stat2_in[0]
    for s in range(1, NZ):
        both = both + stat2_in[s]
    first, second = split_pair(both)
    in_grad[...] = (
        (hat_grad - first / FEATURES - centred * (second / FEATURES)) * inv_std
    ).astype(BF)
    for copy in gains:
        copy.wait_recv()
    g_grad[...] = (gy_in[0] + gy_in[1]) + (gy_in[2] + gy_in[3])
    for copy in biases + returned:
        copy.wait_recv()
    net.drain()


def shards(tokens, gain, w_in, b_in, w_out, cotangent):
    vmem = pl.BlockSpec(memory_space=pltpu.VMEM)
    outs = pl.pallas_call(
        kernel,
        out_shape=(
            jax.ShapeDtypeStruct((SH, W), BF),
            jax.ShapeDtypeStruct((SH, W), BF),
            jax.ShapeDtypeStruct((W, W), BF),
            jax.ShapeDtypeStruct((4 * W, FB), BF),
            jax.ShapeDtypeStruct((4, 1, W), F32),
            jax.ShapeDtypeStruct((1, W), F32),
        ),
        in_specs=[vmem] * 6,
        out_specs=[vmem] * 6,
        scratch_shapes=[
            pltpu.VMEM((2, NZ, 2, SH, W), BF),
            pltpu.VMEM((2, NZ, 2, SH, W), BF),
            pltpu.VMEM((W, W), BF),
            pltpu.VMEM((W, W), BF),
            pltpu.VMEM((W, W), BF),
            pltpu.VMEM((W, W), BF),
            pltpu.VMEM((4, W, FB), BF),
            pltpu.VMEM((W, W), BF),
            pltpu.VMEM((4, W, FB), BF),
            pltpu.VMEM((NZ, SH, LANES), F32),
            pltpu.VMEM((2, CH, W), BF),
            pltpu.VMEM((2, 2, HALF, W), F32),
            pltpu.VMEM((2, 2, CH, W), BF),
            pltpu.VMEM((2, CH, W), F32),
            pltpu.VMEM((2, 2, HALF, W), BF),
            pltpu.VMEM((2, 2, CH, W), BF),
            pltpu.VMEM((2, CH, W), BF),
            pltpu.VMEM((2, CH, W), BF),
            pltpu.VMEM((CH, W), F32),
            pltpu.VMEM((2, 2, NZ, SH, W), F32),
            pltpu.VMEM((2, 2, NZ, SH, W), BF),
            pltpu.VMEM((2, 2, NZ, SH, W), BF),
            pltpu.VMEM((2, 2, NZ, SH, W), BF),
            pltpu.VMEM((2, 2, NZ, SH, W), BF),
            pltpu.VMEM((2, 2, SH, W), F32),
            pltpu.VMEM((2, SH, W), BF),
            pltpu.VMEM((2, SH, W), BF),
            pltpu.VMEM((NZ, SH, LANES), F32),
            pltpu.VMEM((NZ, 1, W), F32),
            pltpu.VMEM((4, 1, W), F32),
            pltpu.SemaphoreType.DMA((COPIES,)),
            pltpu.SemaphoreType.DMA((COPIES,)),
        ],
        compiler_params=pltpu.CompilerParams(
            collective_id=0, has_side_effects=True, vmem_limit_bytes=58 << 20
        ),
        cost_estimate=pl.CostEstimate(
            flops=12 * W * W * W, bytes_accessed=10 * W * W, transcendentals=CH * W
        ),
    )(tokens, gain.reshape(1, W), w_in, b_in.reshape(1, 4 * W), w_out, cotangent)
    y_branch, input_grad, w_in_grad, w_out_grad, bias_grad, gain_grad = outs
    return (
        y_branch,
        input_grad,
        w_in_grad,
        w_out_grad,
        bias_grad.reshape(4 * W),
        gain_grad.reshape(W),
    )


def solution(mesh):
    placed = (
        P(("gy", "gx"), "gz"),
        P("gz"),
        P("gz", ("gx", "gy")),
        P("gx"),
        P("gx", ("gz", "gy")),
        P(("gy", "gx"), "gz"),
    )
    return jax.shard_map(
        shards,
        mesh=mesh,
        in_specs=placed,
        out_specs=(
            P(("gy", "gx"), "gz"),
            P(("gy", "gx"), "gz"),
            P("gz", ("gx", "gy")),
            P("gx", ("gz", "gy")),
            P("gx"),
            P("gz"),
        ),
        check_vma=False,
    )
```

time: 738 us -> 143 us (0.19)
  waiting for transfers between devices: 543 us -> 0 us
  blocking collectives: 142 us -> 0 us
  Pallas kernels: 0 us -> 132 us
  matrix products: 17.9 us -> 0 us
  between operations: 14.2 us -> 0.65 us
    reduce_scatter x4 -> x0, waiting for transfers between devices: 284 us -> none  [the longest x1 84.2 us: shards(): lax.psum_scatter(contract_last(pre_grad_all, w_in).astype(jnp.bfloat16),...]
    all_gather x4 -> x0, waiting for transfers between devices: 257 us -> none  [the longest x1 99.7 us: shards(): normed_all = lax.all_gather(normed, ('gy', 'gx'), axis=0, tiled=True)]
    pallas_call x0 -> x1, Pallas kernels: none -> 132 us  [shards(): pl.pallas_call(kernel, out_shape=(jax.ShapeDtypeStruct((SH, W), BF), jax....]
    psum x3 -> x0, blocking collectives: 102 us -> none  [the longest x1 59.7 us: shards(): gain_grad = lax.psum(jnp.sum(norm_grad * centred, 0), ('gx', 'gy'))]
    all_to_all x1 -> x0, blocking collectives: 23.2 us -> none  [shards(): lax.all_to_all(w_out, 'gy', split_axis=0, concat_axis=1, tiled=True)]
    dot_general x6 -> x0, matrix products: 17.9 us -> none  [the longest x2 6.8 us: contract_last(): lax.dot_general(left_side, right_side, (((1,), (1,)), ((), ())), preferre...]
    all_gather x1 -> x0, blocking collectives: 17.2 us -> none  [shards(): bias_grad = lax.all_gather(bias_term, 'gy', axis=0, tiled=True)]
  transfers between devices with their start and end apart: 9 -> 0, of which waited for: 8 -> 0; matrix products, arithmetic and copies ran while one was open for 4% -> 0% of each run, Pallas kernels for 0% -> 0%
where the time goes in v2:
time: 143 us
  Pallas kernels  132 us (92%)
  local copies, waits for them, and re-layouts  9.23 us (6%)
    pallas_call x1, Pallas kernels, shards(): pl.pallas_call(kernel, out_shape=(jax.ShapeDtypeStruct((SH, W), BF), jax....  132 us
    unnamed x14, local copies, waits for them, and re-layouts  7.96 us

profile of v2, /device:TPU:1, one launch (start us, length us, event | category | flops | bytes accessed | tf_op | source)
XLA Modules:
  0.0 143.1 jit_solution(15922146585884506747)
XLA Ops:
  0.6 1.3 reshape.24.gain
  1.9 2.5 %copy.12.w_out = bf16[3072,192]{1,0:T(8,128)(2,1)} copy(bf16[3072,192]{0,1:T(8,128)(2,1)} %param.10) | data formatting | bytes 2359296 | tf_op args[4]
  4.4 131.9 %shard_map.109 = (bf16[24,768]{1,0:T(8,128)(2,1)}, bf16[24,768]{1,0:T(8,128)(2,1)}, bf16[768,768]{1,0:T(8,128)(2,1)}, bf16[3072,192]{1,0:T(8,128)(2,1)}, f32[4,1,768]{2,1,0:T(1,128)}, /*index=5*/f32[1,768]{1,0:T(1,128)}) custom-call(bf16[24,768]{1,0:T(8,128)(2,1)} %tok.1, f32[1,768]{1,0:T(1,128)} %reshape.24.gain, bf16[768,768]{1,0:T(8,128)(2,1)} %w_in.1, ...), custom_call_target="tpu_custom_call" | custom-call | flops 5435817984 | bytes 5898240 | tf_op jit(solution)/shard_map/pallas_call | solution.py:505
  136.3 1.3 reduce
  137.6 0.0 copy-start.2
  137.6 0.0 copy-start.1
  137.6 0.0 copy-start
  137.6 2.6 %copy.13 = bf16[3072,192]{0,1:T(8,128)(2,1)} copy(bf16[3072,192]{1,0:T(8,128)(2,1)} %get-tuple-element.21) | data formatting | bytes 2359296
  140.2 0.0 copy-done.2
  140.2 0.6 copy.18
  140.8 0.0 copy-done.1
  140.8 0.6 copy.19
  141.5 0.0 copy-done
  141.5 0.0 copy-start.3
  141.5 1.0 copy.20
  142.5 0.0 copy-done.3
  142.5 0.6 copy.21
Async XLA Ops:
  137.6 2.6 %copy-start.2 = (bf16[24,768]{1,0:T(8,128)(2,1)S(1)}, bf16[24,768]{1,0:T(8,128)(2,1)}, u32[]{:S(2)}) copy-start(bf16[24,768]{1,0:T(8,128)(2,1)} %get-tuple-element.30) | copy-start | bytes 110596
  137.6 3.2 %copy-start.1 = (bf16[24,768]{1,0:T(8,128)(2,1)S(1)}, bf16[24,768]{1,0:T(8,128)(2,1)}, u32[]{:S(2)}) copy-start(bf16[24,768]{1,0:T(8,128)(2,1)} %get-tuple-element.31) | copy-start | bytes 110596
  137.6 3.8 %copy-start = (bf16[768,768]{1,0:T(8,128)(2,1)S(1)}, bf16[768,768]{1,0:T(8,128)(2,1)}, u32[]{:S(2)}) copy-start(bf16[768,768]{1,0:T(8,128)(2,1)} %get-tuple-element.32) | copy-start | bytes 3538948
  141.5 1.0 copy-start.3

commit v3 on v2

--- a/solution.py
+++ b/solution.py
@@ -20,14 +20,36 @@
 FB = 192
 TILE = 256
 LANES = 128
-COPIES = 140
+PARTS = (slice(0, W // 2), slice(W // 2, W))
+COPIES = 170
 FEATURES = W * NZ
 ROOT = 0.7978845608028654
 CUBIC = 0.044715
 
 
+class Sent:
+    def __init__(self, copy):
+        self.copy, self.waited = copy, False
+
+    def wait_recv(self):
+        if not self.waited:
+            self.waited = True
+            self.copy.wait_recv()
+
+
+class Local:
+    def __init__(self, copy):
+        self.copy, self.waited = copy, False
+
+    def wait(self):
+        if not self.waited:
+            self.waited = True
+            self.copy.wait()
+
+
 class Net:
-    def __init__(self, send_sems, recv_sems):
+    def __init__(self, send_sems, recv_sems, local_sems):
+        self.local_sems, self.locals = local_sems, []
         self.send_sems, self.recv_sems = send_sems, recv_sems
         self.count = 0
         self.sent = []
@@ -43,12 +65,21 @@
         )
         self.count += 1
         copy.start()
-        self.sent.append(copy)
-        return copy
+        self.sent.append(Sent(copy))
+        return self.sent[-1]
+
+    def local(self, src, dst):
+        copy = pltpu.make_async_copy(src, dst, self.local_sems.at[len(self.locals)])
+        copy.start()
+        self.locals.append(Local(copy))
+        return self.locals[-1]
 
     def drain(self):
-        for copy in self.sent:
-            copy.wait_send()
+        for copy in self.locals:
+            copy.wait()
+        for sent in self.sent:
+            sent.wait_recv()
+            sent.copy.wait_send()
 
 
 def dot(left, right, left_dim, right_dim):
@@ -70,18 +101,18 @@
 
 
 def kernel(
-    tok, gain, w_in, b_in, w_out, cot,
+    tok, gain, w_in_hbm, b_in, w_out, cot,
     y_out, in_grad, w_in_grad, w_out_grad, b_grad, g_grad,
-    g_cot, g_nor, cot_all, nor_all, act_all, pg_all, w_blk, w_full, w_send,
-    stat_in, far, side_f, side_b, own, relay, inbox, yx_out, yx_in, pre,
-    keep, core_out, core_in, z_out, z_in, total, ty_out, ty_in,
+    g_cot, g_tok, cot_all, nor_all, act_all, pg_all, w_in, w_full, w_send, w_in_out,
+    stat_in, stat_all, far, side_f, side_b, own, relay, inbox, yx_out, yx_in, pre,
+    keep, core_out, core_in, z_out, z_in, z_three, z_four, z_two, total, ty_out, ty_in,
     stat2_in, gz_in, gy_in,
-    send_sems, recv_sems,
+    send_sems, recv_sems, local_sems,
 ):
     z, g, q = lax.axis_index("gx"), lax.axis_index("gy"), lax.axis_index("gz")
     yl, c = lax.div(g, 2), lax.rem(g, 2)
     x, h = lax.div(q, 2), lax.rem(q, 2)
-    net = Net(send_sems, recv_sems)
+    net = Net(send_sems, recv_sems, local_sems)
 
     def ring(value, step, size):
         return lax.rem(value + (step + size), size)
@@ -104,6 +135,15 @@
     y_peer = (1 - yl) * 2 + c
     core_peer = yl * 2 + (1 - c)
     h_peer = x * 2 + (1 - h)
+
+    def hidden_of(group):
+        return pl.ds(pl.multiple_of(group * W, W), W)
+
+    def features_of(group):
+        return pl.ds(pl.multiple_of(group * FB, FB), FB)
+
+    load_w_in = net.local(w_in_hbm, w_in)
+    load_w_out = net.local(w_out.at[:, hidden_of(g)], w_full.at[features_of(g)])
 
     barrier = pltpu.get_barrier_semaphore()
     for s in range(1, NZ):
@@ -111,41 +151,58 @@
         pl.semaphore_signal(barrier, inc=1, device_id={"gz": q_at(s)}, device_id_type=MESH)
     for s in range(1, 4):
         pl.semaphore_signal(barrier, inc=1, device_id={"gy": g_at(s)}, device_id_type=MESH)
-    pl.semaphore_wait(barrier, 2 * (NZ - 1) + 3)
-
-    turned = [
-        net.send(
-            w_out.at[pl.ds(pl.multiple_of(g_at(s) * W, W), W)], w_blk.at[g], gy=g_at(s)
-        )
-        for s in range(1, 4)
-    ]
-    g_cot[c, z, yl] = cot[...]
-    cot_y = net.send(g_cot.at[c, z, yl], g_cot.at[c, z, yl], gy=y_peer)
 
     lane = lax.broadcasted_iota(jnp.int32, (SH, LANES), 1)
+    row = lax.broadcasted_iota(jnp.int32, (SH, LANES), 0)
+    MID = LANES // 2
 
     def pair_tile(first, second):
-        return jnp.where(lane < LANES // 2, first, second)
+        return jnp.where(lane < MID, first, second)
 
     def split_pair(both):
-        return both[:, 0:1], both[:, LANES // 2 : LANES // 2 + 1]
+        return both[:, 0:1], both[:, MID : MID + 1]
 
     floats = tok[...].astype(F32)
     stat_in[0] = pair_tile(
         jnp.sum(floats, 1, keepdims=True), jnp.sum(floats * floats, 1, keepdims=True)
     )
+    g_tok[c, z, yl] = tok[...]
+    g_cot[c, z, yl] = cot[...]
+    pl.semaphore_wait(barrier, 2 * (NZ - 1) + 3)
+
     stats = [net.send(stat_in.at[0], stat_in.at[s], gz=q_at(s)) for s in range(1, NZ)]
 
+    class Lane:
+        def __init__(self, which):
+            self.which, self.right, self.left = which, {}, {}
+            self.forward(0, True, True)
+
+        def forward(self, step, right, left):
+            block = g_tok.at[c, z_at(step), self.which]
+            if right:
+                self.right[1 - step] = net.send(block, block, gx=z_at(1))
+            if left:
+                self.left[1 + step] = net.send(block, block, gx=z_at(-1))
+
+        def onward(self, n):
+            self.right[n].wait_recv()
+            self.forward(-n, n < 4, False)
+            if n < 4:
+                self.left[n].wait_recv()
+                self.forward(n, False, n < 3)
+
+    def tok_to_core(step):
+        block = g_tok.at[c, z_at(step)]
+        tok_cores.append(net.send(block, block, gy=core_peer))
+
     class Gather:
-        def __init__(self, buf, first):
-            self.buf, self.first = buf, first
+        def __init__(self, buf):
+            self.buf = buf
+            self.first = net.send(buf.at[c, z, yl], buf.at[c, z, yl], gy=y_peer)
             self.right, self.left, self.cores = {}, {}, []
 
-        def block(self, step):
-            return self.buf.at[c, z_at(step)]
-
         def forward(self, step, right, left):
-            block = self.block(step)
+            block = self.buf.at[c, z_at(step)]
             if right:
                 self.right[1 - step] = net.send(block, block, gx=z_at(1))
             if left:
@@ -156,13 +213,12 @@
             self.first.wait_recv()
             self.forward(0, True, True)
 
-        def from_left(self, n):
+        def onward(self, n):
             self.right[n].wait_recv()
             self.forward(-n, n < 4, False)
-
-        def from_right(self, n):
-            self.left[n].wait_recv()
-            self.forward(n, False, n < 3)
+            if n < 4:
+                self.left[n].wait_recv()
+                self.forward(n, False, n < 3)
 
         def finish(self, whole):
             for copy in self.cores:
@@ -171,9 +227,19 @@
                 piece = self.buf[block % 2, :, block // 2].astype(F32).reshape(CH, W)
                 whole[pl.ds(block * CH, CH), :] = piece.astype(BF)
 
-    cots = Gather(g_cot, cot_y)
+    tok_cores = []
+    tok_y = net.send(g_tok.at[c, z, yl], g_tok.at[c, z, yl], gy=y_peer)
+    near = Lane(yl)
+    cots = Gather(g_cot)
+    turned = [
+        net.send(w_out.at[:, hidden_of(g_at(s))], w_full.at[features_of(g)], gy=g_at(s))
+        for s in range(1, 4)
+    ]
+    tok_y.wait_recv()
+    across = Lane(1 - yl)
+    tok_to_core(0)
+    near.onward(1)
     cots.begin()
-
     for copy in stats:
         copy.wait_recv()
     both = stat_in[0]
@@ -184,34 +250,64 @@
     row_var = row_square / FEATURES - row_mean * row_mean
     inv_std = lax.rsqrt(row_var + epsilon)
 
+    def gain_row():
+        return gain[...].reshape(1, W)
+
     def centre():
         return (tok[...].astype(F32) - row_mean) * inv_std
 
-    g_nor[c, z, yl] = (centre() * gain[...]).astype(BF)
-    nors = Gather(g_nor, net.send(g_nor.at[c, z, yl], g_nor.at[c, z, yl], gy=y_peer))
-
-    cots.from_left(1)
-    cots.from_right(1)
-    nors.begin()
-    cots.from_left(2)
-    cots.from_right(2)
-    nors.from_left(1)
-    nors.from_right(1)
-    cots.from_left(3)
-    cots.from_right(3)
-    nors.from_left(2)
-    nors.from_right(2)
-    cots.from_left(4)
-    nors.from_left(3)
-    nors.from_right(3)
-    nors.from_left(4)
-    nors.finish(nor_all)
+    on_row = lane == row
+    on_mid = lane == row + MID
+
+    def rows_centred(target):
+        packed = stat_all[2 * target + c, z]
+        means = jnp.sum(jnp.where(on_row, packed, 0.0), 1, keepdims=True)
+        scales = jnp.sum(jnp.where(on_mid, packed, 0.0), 1, keepdims=True)
+        return (g_tok[c, z, target].astype(F32) - means) * scales
+
+    stat_all[g, z] = jnp.sum(
+        jnp.where(on_row, row_mean, 0.0) + jnp.where(on_mid, inv_std, 0.0), 0, keepdims=True
+    )
+    stats = [net.send(stat_all.at[g, z], stat_all.at[g, z], gx=z_at(s)) for s in range(1, NZ)]
+
+    across.onward(1)
+    tok_to_core(1)
+    tok_to_core(-1)
+    near.onward(2)
+    for copy in stats:
+        copy.wait_recv()
+    stats = [net.send(stat_all.at[g], stat_all.at[g], gy=g_at(s)) for s in range(1, 4)]
+    across.onward(2)
+    tok_to_core(2)
+    tok_to_core(-2)
+    cots.onward(1)
+    near.onward(3)
+    across.onward(3)
+    tok_to_core(3)
+    tok_to_core(-3)
+    cots.onward(2)
+    near.onward(4)
+    across.onward(4)
+    tok_to_core(-4)
+    for copy in stats:
+        copy.wait_recv()
+    for copy in tok_cores:
+        copy.wait_recv()
+    gains_row = gain_row()
+    for block in range(4):
+        packed = stat_all[block]
+        means = jnp.sum(jnp.where(on_row[None], packed, 0.0), 2, keepdims=True)
+        scales = jnp.sum(jnp.where(on_mid[None], packed, 0.0), 2, keepdims=True)
+        piece = (g_tok[block % 2, :, block // 2].astype(F32) - means) * scales
+        nor_all[pl.ds(block * CH, CH), :] = (
+            (piece * gains_row[None]).reshape(CH, W).astype(BF)
+        )
 
     class HiddenSum:
         def __init__(self, n, product):
             self.n, self.product = n, product
 
-        def begin(self):
+        def begin(self, between=()):
             n = self.n
 
             def far_tile(cols):
@@ -222,6 +318,8 @@
                 net.send(far.at[n, pl.ds(0, HALF)], relay.at[n, 0], gz=x_dev(1)),
                 net.send(far.at[n, pl.ds(HALF, HALF)], relay.at[n, 1], gz=x_dev(-1)),
             ]
+            for action in between:
+                action()
             self.raw = []
             for side, step in enumerate((1, -1)):
 
@@ -283,19 +381,16 @@
             return yx_out[n, rows, :].astype(F32) + yx_in[n, rows, :].astype(F32)
 
     pres = HiddenSum(0, lambda k, cols: dot(nor_all[rows_of(k), :], w_in[:, cols], 1, 0))
-    grads = HiddenSum(1, lambda k, cols: dot(cot_all[rows_of(k), :], w_full[cols, :], 1, 1))
-
-    pres.begin()
-
+    grads = HiddenSum(1, lambda k, cols: dot(cot_all[rows_of(k), :], w_full[:, cols], 1, 0))
+
+    load_w_in.wait()
+    pres.begin([lambda: cots.onward(3)])
+
+    cots.onward(4)
     cots.finish(cot_all)
-    w_blk[g] = w_out[pl.ds(pl.multiple_of(g * W, W), W), :]
     for copy in turned:
         copy.wait_recv()
-
-    def assemble(rows):
-        w_full[rows, :] = jnp.concatenate([w_blk[i, rows, :] for i in range(4)], axis=1)
-
-    tiles(assemble)
+    load_w_out.wait()
 
     pres.relayed()
     grads.begin()
@@ -322,6 +417,97 @@
         def finish(self):
             for copy in self.onwards:
                 copy.wait_recv()
+
+    class FeatureSum:
+        def __init__(self, n, product):
+            self.n, self.product = n, product
+            self.cores, self.three, self.four, self.last_hops = {}, {}, {}, {}
+
+        def target(self, order):
+            return lax.div(x, 2) if order == 0 else 1 - lax.div(x, 2)
+
+        def products(self, order):
+            n, j = self.n, self.target(order)
+
+            def send_tile(cols):
+                value = self.product(2 * j + (1 - c), cols)
+                core_out[n, order, :, :, cols] = value.reshape(NZ, SH, TILE).astype(BF)
+
+            tiles(send_tile)
+            self.cores[order] = net.send(
+                core_out.at[n, order], core_in.at[n, order], gy=core_peer
+            )
+
+            def keep_tile(cols):
+                value = self.product(2 * j + c, cols)
+                keep[n, order, :, :, cols] = value.reshape(NZ, SH, TILE)
+
+            tiles(keep_tile)
+
+        def scatter(self, order):
+            n = self.n
+            self.cores[order].wait_recv()
+
+            def add_one(i, carry):
+                value = keep[n, order, i] + core_in[n, order, i].astype(F32)
+                keep[n, order, i] = value
+                z_out[n, order, i] = value.astype(BF)
+                return carry
+
+            lax.fori_loop(0, NZ, add_one, 0)
+            out, sides = z_out.at[n, order], tuple(enumerate((1, -1)))
+            self.three[order] = [
+                net.send(out.at[z_at(3 * d)], z_three.at[n, order, i], gx=z_at(d))
+                for i, d in sides
+            ]
+            self.four[order] = [
+                net.send(
+                    out.at[z_at(4), :, part], z_four.at[n, order, i, :, part], gx=z_at(2 * d)
+                )
+                for (i, d), part in zip(sides, PARTS)
+            ]
+            self.last_hops[order] = [
+                net.send(out.at[z_at(d)], z_in.at[n, order, i], gx=z_at(d)) for i, d in sides
+            ]
+
+        def relay(self, order):
+            n = self.n
+            for i, d in enumerate((1, -1)):
+                self.three[order][i].wait_recv()
+                self.four[order][i].wait_recv()
+                dest = z_at(2 * d)
+                for k, part in enumerate(PARTS):
+                    value = keep[n, order, dest, :, part]
+                    value = value + z_three[n, order, i, :, part].astype(F32)
+                    if k == i:
+                        value = value + z_four[n, order, i, :, part].astype(F32)
+                    z_two[n, order, i, :, part] = value.astype(BF)
+                self.last_hops[order].append(
+                    net.send(z_two.at[n, order, i], z_in.at[n, order, 2 + i], gx=dest)
+                )
+
+        def collect(self, order):
+            n = self.n
+            for copy in self.last_hops[order]:
+                copy.wait_recv()
+            value = keep[n, order, z]
+            for s in range(4):
+                value = value + z_in[n, order, s].astype(F32)
+            total[n, order] = value
+
+        def exchange(self):
+            n = self.n
+            here = lax.rem(lax.div(x, 2) + yl, 2)
+            ty_out[n] = total[n, 1 - here].astype(BF)
+            self.last = net.send(ty_out.at[n], ty_in.at[n], gy=y_peer)
+            self.here = here
+
+        def result(self):
+            self.last.wait_recv()
+            return total[self.n, self.here] + ty_in[self.n].astype(F32)
+
+    ys = FeatureSum(0, lambda k, cols: dot(act_all[rows_of(k), :], w_full[cols, :], 1, 1))
+    norms = FeatureSum(1, lambda k, cols: dot(pg_all[rows_of(k), :], w_in[cols, :], 1, 1))
 
     STEP = 32
     for part_index in range(2):
@@ -345,6 +531,7 @@
 
     grads.pair_up()
     acts.onward()
+    ys.products(0)
     for part_index in range(2):
         grads.pairs[part_index].wait_recv()
 
@@ -359,95 +546,31 @@
         lax.fori_loop(0, HALF // STEP, backward, 0)
     pgs = HiddenGather(pg_all)
 
-    class FeatureSum:
-        def __init__(self, n, product):
-            self.n, self.product = n, product
-            self.cores, self.spread = {}, {}
-
-        def products(self, order):
-            n = self.n
-            j = lax.div(x, 2) if order == 0 else 1 - lax.div(x, 2)
-
-            def send_tile(cols):
-                value = self.product(2 * j + (1 - c), cols)
-                core_out[n, order, :, :, cols] = value.reshape(NZ, SH, TILE).astype(BF)
-
-            tiles(send_tile)
-            self.cores[order] = net.send(
-                core_out.at[n, order], core_in.at[n, order], gy=core_peer
-            )
-
-            def keep_tile(cols):
-                value = self.product(2 * j + c, cols)
-                keep[n, order, :, :, cols] = value.reshape(NZ, SH, TILE)
-
-            tiles(keep_tile)
-
-        def scatter(self, order):
-            n = self.n
-            self.cores[order].wait_recv()
-
-            def add_one(i, carry):
-                value = keep[n, order, i] + core_in[n, order, i].astype(F32)
-                keep[n, order, i] = value
-                z_out[n, order, i] = value.astype(BF)
-                return carry
-
-            lax.fori_loop(0, NZ, add_one, 0)
-            self.spread[order] = [
-                net.send(z_out.at[n, order, z_at(s)], z_in.at[n, order, s - 1], gx=z_at(s))
-                for s in range(1, NZ)
-            ]
-
-        def collect(self, order):
-            n = self.n
-            for copy in self.spread[order]:
-                copy.wait_recv()
-            value = keep[n, order, z]
-            for s in range(NZ - 1):
-                value = value + z_in[n, order, s].astype(F32)
-            total[n, order] = value
-
-        def exchange(self):
-            n = self.n
-            here = lax.rem(lax.div(x, 2) + yl, 2)
-            ty_out[n] = total[n, 1 - here].astype(BF)
-            self.last = net.send(ty_out.at[n], ty_in.at[n], gy=y_peer)
-            self.here = here
-
-        def result(self):
-            self.last.wait_recv()
-            return total[self.n, self.here] + ty_in[self.n].astype(F32)
-
-    ys = FeatureSum(0, lambda k, cols: dot(act_all[rows_of(k), :], w_full[:, cols], 1, 0))
-    norms = FeatureSum(1, lambda k, cols: dot(pg_all[rows_of(k), :], w_in[cols, :], 1, 1))
-
-    ys.products(0)
     ys.scatter(0)
     acts.finish()
     ys.products(1)
+    ys.relay(0)
+
+    def w_out_tile(rows):
+        w_send[rows, :] = dot(cot_all[:, rows], act_all[...], 0, 0).astype(BF)
+
+    tiles(w_out_tile)
+    for s in range(1, 4):
+        net.send(
+            w_send.at[features_of(g_at(s))], w_out_grad.at[:, hidden_of(g)], gy=g_at(s)
+        )
+    net.local(w_send.at[features_of(g)], w_out_grad.at[:, hidden_of(g)])
     ys.scatter(1)
-
-    def w_out_tile(rows):
-        value = dot(act_all[:, rows], cot_all[...], 0, 0)
-        for i in range(4):
-            w_send[i, rows, :] = value[:, i * FB : (i + 1) * FB].astype(BF)
-
-    tiles(w_out_tile)
-    own_rows = pl.ds(pl.multiple_of(g * W, W), W)
-    returned = [
-        net.send(w_send.at[g_at(s)], w_out_grad.at[own_rows], gy=g_at(s)) for s in range(1, 4)
-    ]
-    w_out_grad[own_rows, :] = w_send[g]
-
     pgs.onward()
+    norms.products(0)
+    ys.relay(1)
+    norms.scatter(0)
     ys.collect(0)
-    norms.products(0)
-    norms.scatter(0)
     ys.collect(1)
     ys.exchange()
     pgs.finish()
     norms.products(1)
+    norms.relay(0)
     norms.scatter(1)
 
     def bias_sum(i, carry):
@@ -458,24 +581,29 @@
     biases = [net.send(b_grad.at[g], b_grad.at[g], gy=g_at(s)) for s in range(1, 4)]
 
     def w_in_tile(rows):
-        w_in_grad[rows, :] = dot(nor_all[:, rows], pg_all[...], 0, 0).astype(BF)
+        w_in_out[rows, :] = dot(nor_all[:, rows], pg_all[...], 0, 0).astype(BF)
 
     tiles(w_in_tile)
-
+    net.local(w_in_out, w_in_grad)
+
+    norms.relay(1)
     norms.collect(0)
     norms.collect(1)
     norms.exchange()
+    gz_in[z] = sum(
+        jnp.sum(total[1, order] * rows_centred(norms.target(order)), 0, keepdims=True)
+        for order in range(2)
+    )
+    gains = [net.send(gz_in.at[z], gz_in.at[z], gx=z_at(s)) for s in range(1, NZ)]
     y_out[...] = ys.result().astype(BF)
 
     norm_grad = norms.result()
     centred = centre()
-    hat_grad = norm_grad * gain[...]
+    hat_grad = norm_grad * gain_row()
     stat2_in[0] = pair_tile(
         jnp.sum(hat_grad, 1, keepdims=True), jnp.sum(hat_grad * centred, 1, keepdims=True)
     )
     stats2 = [net.send(stat2_in.at[0], stat2_in.at[s], gz=q_at(s)) for s in range(1, NZ)]
-    gz_in[z] = jnp.sum(norm_grad * centred, 0, keepdims=True)
-    gains = [net.send(gz_in.at[z], gz_in.at[z], gx=z_at(s)) for s in range(1, NZ)]
     for copy in gains:
         copy.wait_recv()
     value = gz_in[0]
@@ -495,25 +623,40 @@
     for copy in gains:
         copy.wait_recv()
     g_grad[...] = (gy_in[0] + gy_in[1]) + (gy_in[2] + gy_in[3])
-    for copy in biases + returned:
-        copy.wait_recv()
     net.drain()
+
+
+def hand_over(*refs):
+    ins, outs, held, sems = refs[:6], refs[6:12], refs[12:17], refs[17]
+    order = (2, 3, 0, 1, 4)
+    first = {i: pltpu.make_async_copy(ins[i], held[i], sems.at[i]) for i in order}
+    second = {i: pltpu.make_async_copy(held[i], outs[i], sems.at[5 + i]) for i in order}
+    for i in order:
+        first[i].start()
+    outs[5][...] = ins[5][...].reshape(W)
+    for i in order:
+        first[i].wait()
+        second[i].start()
+    for i in order:
+        second[i].wait()
 
 
 def shards(tokens, gain, w_in, b_in, w_out, cotangent):
     vmem = pl.BlockSpec(memory_space=pltpu.VMEM)
+    hbm = pl.BlockSpec(memory_space=pl.ANY)
+    results = (
+        jax.ShapeDtypeStruct((SH, W), BF),
+        jax.ShapeDtypeStruct((SH, W), BF),
+        jax.ShapeDtypeStruct((W, W), BF),
+        jax.ShapeDtypeStruct((FB, 4 * W), BF),
+        jax.ShapeDtypeStruct((4, 1, W), F32),
+        jax.ShapeDtypeStruct((1, W), F32),
+    )
     outs = pl.pallas_call(
         kernel,
-        out_shape=(
-            jax.ShapeDtypeStruct((SH, W), BF),
-            jax.ShapeDtypeStruct((SH, W), BF),
-            jax.ShapeDtypeStruct((W, W), BF),
-            jax.ShapeDtypeStruct((4 * W, FB), BF),
-            jax.ShapeDtypeStruct((4, 1, W), F32),
-            jax.ShapeDtypeStruct((1, W), F32),
-        ),
-        in_specs=[vmem] * 6,
-        out_specs=[vmem] * 6,
+        out_shape=results,
+        in_specs=[vmem, vmem, hbm, vmem, hbm, vmem],
+        out_specs=[vmem, vmem, hbm, hbm, vmem, vmem],
         scratch_shapes=[
             pltpu.VMEM((2, NZ, 2, SH, W), BF),
             pltpu.VMEM((2, NZ, 2, SH, W), BF),
@@ -521,10 +664,12 @@
             pltpu.VMEM((W, W), BF),
             pltpu.VMEM((W, W), BF),
             pltpu.VMEM((W, W), BF),
-            pltpu.VMEM((4, W, FB), BF),
             pltpu.VMEM((W, W), BF),
-            pltpu.VMEM((4, W, FB), BF),
+            pltpu.VMEM((W, W), BF),
+            pltpu.VMEM((W, W), BF),
+            pltpu.VMEM((W, W), BF),
             pltpu.VMEM((NZ, SH, LANES), F32),
+            pltpu.VMEM((4, NZ, 1, LANES), F32),
             pltpu.VMEM((2, CH, W), BF),
             pltpu.VMEM((2, 2, HALF, W), F32),
             pltpu.VMEM((2, 2, CH, W), BF),
@@ -538,7 +683,10 @@
             pltpu.VMEM((2, 2, NZ, SH, W), BF),
             pltpu.VMEM((2, 2, NZ, SH, W), BF),
             pltpu.VMEM((2, 2, NZ, SH, W), BF),
-            pltpu.VMEM((2, 2, NZ, SH, W), BF),
+            pltpu.VMEM((2, 2, 4, SH, W), BF),
+            pltpu.VMEM((2, 2, 2, SH, W), BF),
+            pltpu.VMEM((2, 2, 2, SH, W), BF),
+            pltpu.VMEM((2, 2, 2, SH, W), BF),
             pltpu.VMEM((2, 2, SH, W), F32),
             pltpu.VMEM((2, SH, W), BF),
             pltpu.VMEM((2, SH, W), BF),
@@ -547,6 +695,7 @@
             pltpu.VMEM((4, 1, W), F32),
             pltpu.SemaphoreType.DMA((COPIES,)),
             pltpu.SemaphoreType.DMA((COPIES,)),
+            pltpu.SemaphoreType.DMA((4,)),
         ],
         compiler_params=pltpu.CompilerParams(
             collective_id=0, has_side_effects=True, vmem_limit_bytes=58 << 20
@@ -554,15 +703,22 @@
         cost_estimate=pl.CostEstimate(
             flops=12 * W * W * W, bytes_accessed=10 * W * W, transcendentals=CH * W
         ),
-    )(tokens, gain.reshape(1, W), w_in, b_in.reshape(1, 4 * W), w_out, cotangent)
-    y_branch, input_grad, w_in_grad, w_out_grad, bias_grad, gain_grad = outs
+    )(tokens, gain, w_in, b_in.reshape(1, 4 * W), w_out.T, cotangent)
+    y_branch, input_grad, w_in_grad, w_out_grad, bias_grad, gain_grad = pl.pallas_call(
+        hand_over,
+        out_shape=results[:5] + (jax.ShapeDtypeStruct((W,), F32),),
+        in_specs=[hbm] * 5 + [vmem],
+        out_specs=[hbm] * 5 + [vmem],
+        scratch_shapes=[pltpu.VMEM(one.shape, one.dtype) for one in results[:5]]
+        + [pltpu.SemaphoreType.DMA((10,))],
+    )(*outs)
     return (
         y_branch,
         input_grad,
         w_in_grad,
-        w_out_grad,
+        w_out_grad.T,
         bias_grad.reshape(4 * W),
-        gain_grad.reshape(W),
+        gain_grad,
     )
 
 

time: 143 us -> 107 us (0.75)
  Pallas kernels: 132 us -> 106 us
  local copies, waits for them, and re-layouts: 9.23 us -> 0 us
    pallas_call x1 -> x2, Pallas kernels: 132 us -> 106 us  [the longest x1 102 us: shards(): pl.pallas_call(kernel, out_shape=results, in_specs=[vmem, vmem, hbm, vmem...]
    unnamed x14 -> x0, local copies, waits for them, and re-layouts: 7.96 us -> none
where the time goes in v3:
time: 107 us; the launch traced here: 106 us
  Pallas kernels  106 us (99%)
    pallas_call x1, Pallas kernels, shards(): pl.pallas_call(kernel, out_shape=results, in_specs=[vmem, vmem, hbm, vmem...  102 us
    pallas_call x1, Pallas kernels, shards(): pl.pallas_call(hand_over, out_shape=results[:5] + (jax.ShapeDtypeStruct((...  4.03 us

profile of v3, /device:TPU:1, one launch (start us, length us, event | category | flops | bytes accessed | tf_op | source)
XLA Modules:
  0.0 106.3 jit_solution(12186583857763303415)
XLA Ops:
  0.6 101.6 %shard_map.109 = (bf16[24,768]{1,0:T(8,128)(2,1)}, bf16[24,768]{1,0:T(8,128)(2,1)}, bf16[768,768]{1,0:T(8,128)(2,1)}, bf16[192,3072]{1,0:T(8,128)(2,1)}, f32[4,1,768]{2,1,0:T(1,128)}, /*index=5*/f32[1,768]{1,0:T(1,128)}) custom-call(bf16[24,768]{1,0:T(8,128)(2,1)} %tok.1, f32[768]{0:T(1024)} %gain.1, bf16[768,768]{1,0:T(8,128)(2,1)} %w_in_hbm.1, ...), custom_call_target="tpu_custom_call" | custom-call | flops 5435817984 | bytes 5898240 | tf_op jit(solution)/shard_map/pallas_call | solution.py:655
  102.2 4.0 %shard_map.110 = (bf16[24,768]{1,0:T(8,128)(2,1)}, bf16[24,768]{1,0:T(8,128)(2,1)}, bf16[768,768]{1,0:T(8,128)(2,1)}, bf16[192,3072]{1,0:T(8,128)(2,1)}, f32[4,1,768]{2,1,0:T(1,128)}, /*index=5*/f32[768]{0:T(1024)}) custom-call(bf16[24,768]{1,0:T(8,128)(2,1)} %get-tuple-element.18.refs_0_, bf16[24,768]{1,0:T(8,128)(2,1)} %get-tuple-element.19.refs_1_, ...), custom_call_target="tpu_custom_call" | custom-call | tf_op jit(solution)/shard_map/pallas_call | solution.py:707

commit v4 on v3

--- a/solution.py
+++ b/solution.py
@@ -16,12 +16,15 @@
 W = 768
 CH = 192
 HALF = CH // 2
+QUART = HALF // 2
+OFFSETS = (0, 1, -1, 2, -2, 3, -3, 4)
+PLACE = {d: i for i, d in enumerate(OFFSETS)}
 SH = 24
 FB = 192
 TILE = 256
 LANES = 128
 PARTS = (slice(0, W // 2), slice(W // 2, W))
-COPIES = 170
+COPIES = 210
 FEATURES = W * NZ
 ROOT = 0.7978845608028654
 CUBIC = 0.044715
@@ -88,8 +91,12 @@
     )
 
 
-def rows_of(chunk):
-    return pl.ds(pl.multiple_of(chunk * CH, CH), CH)
+def rows_of(half, chunk):
+    return pl.ds(pl.multiple_of(half * (4 * HALF) + chunk * HALF, HALF), HALF)
+
+
+def both_halves(ref, chunk):
+    return jnp.concatenate([ref[rows_of(half, chunk), :] for half in range(2)], axis=0)
 
 
 def tiles(body, count=W // TILE, size=TILE):
@@ -106,7 +113,7 @@
     g_cot, g_tok, cot_all, nor_all, act_all, pg_all, w_in, w_full, w_send, w_in_out,
     stat_in, stat_all, far, side_f, side_b, own, relay, inbox, yx_out, yx_in, pre,
     keep, core_out, core_in, z_out, z_in, z_three, z_four, z_two, total, ty_out, ty_in,
-    stat2_in, gz_in, gy_in,
+    stat2_in, stat2_out, gz_in, gy_in,
     send_sems, recv_sems, local_sems,
 ):
     z, g, q = lax.axis_index("gx"), lax.axis_index("gy"), lax.axis_index("gz")
@@ -149,6 +156,8 @@
     for s in range(1, NZ):
         pl.semaphore_signal(barrier, inc=1, device_id={"gx": z_at(s)}, device_id_type=MESH)
         pl.semaphore_signal(barrier, inc=1, device_id={"gz": q_at(s)}, device_id_type=MESH)
+        where = {"gy": y_peer, "gz": q_at(s)}
+        pl.semaphore_signal(barrier, inc=1, device_id=where, device_id_type=MESH)
     for s in range(1, 4):
         pl.semaphore_signal(barrier, inc=1, device_id={"gy": g_at(s)}, device_id_type=MESH)
 
@@ -168,7 +177,7 @@
     )
     g_tok[c, z, yl] = tok[...]
     g_cot[c, z, yl] = cot[...]
-    pl.semaphore_wait(barrier, 2 * (NZ - 1) + 3)
+    pl.semaphore_wait(barrier, 3 * (NZ - 1) + 3)
 
     stats = [net.send(stat_in.at[0], stat_in.at[s], gz=q_at(s)) for s in range(1, NZ)]
 
@@ -191,9 +200,19 @@
                 self.left[n].wait_recv()
                 self.forward(n, False, n < 3)
 
+    def normalise(half):
+        offsets = OFFSETS[4 * half : 4 * half + 4]
+        for d in offsets:
+            tok_cores[-4 if d == 4 else d].wait_recv()
+        for group in range(4):
+            rows = [
+                centred_rows(group // 2, group % 2, z_at(d)) * gain_row() for d in offsets
+            ]
+            nor_all[rows_of(half, group), :] = jnp.concatenate(rows, 0).astype(BF)
+
     def tok_to_core(step):
         block = g_tok.at[c, z_at(step)]
-        tok_cores.append(net.send(block, block, gy=core_peer))
+        tok_cores[step] = net.send(block, block, gy=core_peer)
 
     class Gather:
         def __init__(self, buf):
@@ -223,18 +242,28 @@
         def finish(self, whole):
             for copy in self.cores:
                 copy.wait_recv()
-            for block in range(4):
-                piece = self.buf[block % 2, :, block // 2].astype(F32).reshape(CH, W)
-                whole[pl.ds(block * CH, CH), :] = piece.astype(BF)
-
-    tok_cores = []
+            for half in range(2):
+                for group in range(4):
+                    piece = self.buf.at[group % 2, :, group // 2]
+                    rows = [
+                        piece[z_at(d)].astype(F32) for d in OFFSETS[4 * half : 4 * half + 4]
+                    ]
+                    whole[rows_of(half, group), :] = jnp.concatenate(rows, 0).astype(BF)
+
+    tok_cores = {}
     tok_y = net.send(g_tok.at[c, z, yl], g_tok.at[c, z, yl], gy=y_peer)
     near = Lane(yl)
     cots = Gather(g_cot)
-    turned = [
-        net.send(w_out.at[:, hidden_of(g_at(s))], w_full.at[features_of(g)], gy=g_at(s))
-        for s in range(1, 4)
-    ]
+
+    def turn(half):
+        part = pl.ds(half * (FB // 2), FB // 2)
+        rows = pl.ds(pl.multiple_of(g * FB + half * (FB // 2), FB // 2), FB // 2)
+        return [
+            net.send(w_out.at[part, hidden_of(g_at(s))], w_full.at[rows], gy=g_at(s))
+            for s in range(1, 4)
+        ]
+
+    turned = turn(0)
     tok_y.wait_recv()
     across = Lane(1 - yl)
     tok_to_core(0)
@@ -259,15 +288,19 @@
     on_row = lane == row
     on_mid = lane == row + MID
 
-    def rows_centred(target):
-        packed = stat_all[2 * target + c, z]
-        means = jnp.sum(jnp.where(on_row, packed, 0.0), 1, keepdims=True)
-        scales = jnp.sum(jnp.where(on_mid, packed, 0.0), 1, keepdims=True)
-        return (g_tok[c, z, target].astype(F32) - means) * scales
-
-    stat_all[g, z] = jnp.sum(
-        jnp.where(on_row, row_mean, 0.0) + jnp.where(on_mid, inv_std, 0.0), 0, keepdims=True
-    )
+    def centred_rows(low, core, where):
+        means, scales = unpack(stat_all[2 * low + core, where])
+        return (g_tok[core, where, low].astype(F32) - means) * scales
+
+    def pack(first, second):
+        both = jnp.where(on_row, first, 0.0) + jnp.where(on_mid, second, 0.0)
+        return jnp.sum(both, 0, keepdims=True)
+
+    def unpack(packed):
+        first = jnp.sum(jnp.where(on_row, packed, 0.0), 1, keepdims=True)
+        return first, jnp.sum(jnp.where(on_mid, packed, 0.0), 1, keepdims=True)
+
+    stat_all[g, z] = pack(row_mean, inv_std)
     stats = [net.send(stat_all.at[g, z], stat_all.at[g, z], gx=z_at(s)) for s in range(1, NZ)]
 
     across.onward(1)
@@ -277,46 +310,30 @@
     for copy in stats:
         copy.wait_recv()
     stats = [net.send(stat_all.at[g], stat_all.at[g], gy=g_at(s)) for s in range(1, 4)]
+    turned += turn(1)
     across.onward(2)
     tok_to_core(2)
     tok_to_core(-2)
     cots.onward(1)
     near.onward(3)
-    across.onward(3)
-    tok_to_core(3)
-    tok_to_core(-3)
-    cots.onward(2)
-    near.onward(4)
-    across.onward(4)
-    tok_to_core(-4)
     for copy in stats:
         copy.wait_recv()
-    for copy in tok_cores:
-        copy.wait_recv()
-    gains_row = gain_row()
-    for block in range(4):
-        packed = stat_all[block]
-        means = jnp.sum(jnp.where(on_row[None], packed, 0.0), 2, keepdims=True)
-        scales = jnp.sum(jnp.where(on_mid[None], packed, 0.0), 2, keepdims=True)
-        piece = (g_tok[block % 2, :, block // 2].astype(F32) - means) * scales
-        nor_all[pl.ds(block * CH, CH), :] = (
-            (piece * gains_row[None]).reshape(CH, W).astype(BF)
-        )
-
     class HiddenSum:
-        def __init__(self, n, product):
-            self.n, self.product = n, product
+        def __init__(self, n, half, product):
+            self.n, self.half, self.product = 2 * n + half, half, product
 
         def begin(self, between=()):
-            n = self.n
+            n, half = self.n, self.half
 
             def far_tile(cols):
-                far[n, :, cols] = self.product(x_at(2), cols).astype(BF)
+                far[n, :, cols] = self.product(half, x_at(2), cols).astype(BF)
 
             tiles(far_tile)
             self.relays = [
-                net.send(far.at[n, pl.ds(0, HALF)], relay.at[n, 0], gz=x_dev(1)),
-                net.send(far.at[n, pl.ds(HALF, HALF)], relay.at[n, 1], gz=x_dev(-1)),
+                net.send(
+                    far.at[n, pl.ds(side * QUART, QUART)], relay.at[n, side], gz=x_dev(step)
+                )
+                for side, step in enumerate((1, -1))
             ]
             for action in between:
                 action()
@@ -324,21 +341,21 @@
             for side, step in enumerate((1, -1)):
 
                 def side_tile(cols):
-                    value = self.product(x_at(step), cols)
-                    side_f[n, side, :, cols] = value[side * HALF : (side + 1) * HALF]
+                    value = self.product(half, x_at(step), cols)
+                    side_f[n, side, :, cols] = value[side * QUART : (side + 1) * QUART]
                     other = 1 - side
-                    side_b[n, side, pl.ds(other * HALF, HALF), cols] = value[
-                        other * HALF : (other + 1) * HALF
+                    side_b[n, side, pl.ds(other * QUART, QUART), cols] = value[
+                        other * QUART : (other + 1) * QUART
                     ].astype(BF)
 
                 tiles(side_tile)
-                part = pl.ds((1 - side) * HALF, HALF)
+                part = pl.ds((1 - side) * QUART, QUART)
                 self.raw.append(
                     net.send(side_b.at[n, side, part], inbox.at[n, side, part], gz=x_dev(step))
                 )
 
             def own_tile(cols):
-                own[n, :, cols] = self.product(x, cols)
+                own[n, :, cols] = self.product(half, x, cols)
 
             tiles(own_tile)
 
@@ -347,7 +364,7 @@
             self.summed = []
             for side, step in enumerate((1, -1)):
                 self.relays[side].wait_recv()
-                part = pl.ds(side * HALF, HALF)
+                part = pl.ds(side * QUART, QUART)
 
                 def add_tile(cols):
                     value = side_f[n, side, :, cols] + relay[n, side, :, cols].astype(F32)
@@ -360,63 +377,81 @@
 
         def pair_up(self):
             n = self.n
-            self.pairs = []
-            for part_index in range(2):
-                part = pl.ds(part_index * HALF, HALF)
-                self.summed[part_index].wait_recv()
-                self.raw[1 - part_index].wait_recv()
-
-                def add_tile(cols):
-                    value = own[n, part, cols] + inbox[n, 0, part, cols].astype(F32)
-                    value = value + inbox[n, 1, part, cols].astype(F32)
-                    yx_out[n, part, cols] = value.astype(BF)
-
-                tiles(add_tile)
-                self.pairs.append(
-                    net.send(yx_out.at[n, part], yx_in.at[n, part], gz=h_peer)
-                )
+            for copy in self.raw + self.summed:
+                copy.wait_recv()
+
+            def add_tile(cols):
+                value = own[n, :, cols] + inbox[n, 0, :, cols].astype(F32)
+                yx_out[n, :, cols] = (value + inbox[n, 1, :, cols].astype(F32)).astype(BF)
+
+            tiles(add_tile)
+            self.pair = net.send(yx_out.at[n], yx_in.at[n], gz=h_peer)
 
         def total(self, rows):
             n = self.n
             return yx_out[n, rows, :].astype(F32) + yx_in[n, rows, :].astype(F32)
 
-    pres = HiddenSum(0, lambda k, cols: dot(nor_all[rows_of(k), :], w_in[:, cols], 1, 0))
-    grads = HiddenSum(1, lambda k, cols: dot(cot_all[rows_of(k), :], w_full[:, cols], 1, 0))
-
+    def pre_product(half, k, cols):
+        return dot(nor_all[rows_of(half, k), :], w_in[:, cols], 1, 0)
+
+    def grad_product(half, k, cols):
+        return dot(cot_all[rows_of(half, k), :], w_full[:, cols], 1, 0)
+
+    pres = [HiddenSum(0, half, pre_product) for half in range(2)]
+    grads = [HiddenSum(1, half, grad_product) for half in range(2)]
+
+    def across_three():
+        across.onward(3)
+        tok_to_core(3)
+        tok_to_core(-3)
+
+    def cots_two():
+        cots.onward(2)
+
+    normalise(0)
     load_w_in.wait()
-    pres.begin([lambda: cots.onward(3)])
-
+    pres[0].begin([across_three, cots_two])
+    near.onward(4)
+    across.onward(4)
+    tok_to_core(-4)
+    normalise(1)
+    pres[0].relayed()
+    pres[1].begin([lambda: cots.onward(3)])
+    pres[0].pair_up()
     cots.onward(4)
+    pres[1].relayed()
     cots.finish(cot_all)
     for copy in turned:
         copy.wait_recv()
     load_w_out.wait()
-
-    pres.relayed()
-    grads.begin()
-    pres.pair_up()
-    grads.relayed()
+    grads[0].begin()
 
     bias = b_in[:, pl.ds(pl.multiple_of(g * W, W), W)]
-    mine = pl.multiple_of(x * CH, CH)
 
     class HiddenGather:
         def __init__(self, whole):
-            self.whole = whole
-            rows = whole.at[pl.ds(mine, CH)]
-            self.sides = [net.send(rows, rows, gz=x_dev(step)) for step in (1, -1)]
+            self.whole, self.sides, self.onwards = whole, {}, []
+
+        def begin(self, half):
+            rows = self.whole.at[rows_of(half, x)]
+            for side, step in enumerate((1, -1)):
+                self.sides[side, half] = net.send(rows, rows, gz=x_dev(step))
 
         def onward(self):
-            self.onwards = []
             for side, step in enumerate((1, -1)):
-                self.sides[side].wait_recv()
-                start = pl.multiple_of(x_at(-step) * CH + side * HALF, HALF)
-                rows = self.whole.at[pl.ds(start, HALF)]
+                self.sides[side, side].wait_recv()
+                rows = self.whole.at[rows_of(side, x_at(-step))]
                 self.onwards.append(net.send(rows, rows, gz=x_dev(step)))
+
+        def neighbours(self):
+            for copy in self.sides.values():
+                copy.wait_recv()
 
         def finish(self):
             for copy in self.onwards:
                 copy.wait_recv()
+
+    acts, pgs = HiddenGather(act_all), HiddenGather(pg_all)
 
     class FeatureSum:
         def __init__(self, n, product):
@@ -457,17 +492,17 @@
             lax.fori_loop(0, NZ, add_one, 0)
             out, sides = z_out.at[n, order], tuple(enumerate((1, -1)))
             self.three[order] = [
-                net.send(out.at[z_at(3 * d)], z_three.at[n, order, i], gx=z_at(d))
+                net.send(out.at[PLACE[3 * d]], z_three.at[n, order, i], gx=z_at(d))
                 for i, d in sides
             ]
             self.four[order] = [
                 net.send(
-                    out.at[z_at(4), :, part], z_four.at[n, order, i, :, part], gx=z_at(2 * d)
+                    out.at[PLACE[4], :, part], z_four.at[n, order, i, :, part], gx=z_at(2 * d)
                 )
                 for (i, d), part in zip(sides, PARTS)
             ]
             self.last_hops[order] = [
-                net.send(out.at[z_at(d)], z_in.at[n, order, i], gx=z_at(d)) for i, d in sides
+                net.send(out.at[PLACE[d]], z_in.at[n, order, i], gx=z_at(d)) for i, d in sides
             ]
 
         def relay(self, order):
@@ -475,22 +510,21 @@
             for i, d in enumerate((1, -1)):
                 self.three[order][i].wait_recv()
                 self.four[order][i].wait_recv()
-                dest = z_at(2 * d)
                 for k, part in enumerate(PARTS):
-                    value = keep[n, order, dest, :, part]
+                    value = keep[n, order, PLACE[2 * d], :, part]
                     value = value + z_three[n, order, i, :, part].astype(F32)
                     if k == i:
                         value = value + z_four[n, order, i, :, part].astype(F32)
                     z_two[n, order, i, :, part] = value.astype(BF)
                 self.last_hops[order].append(
-                    net.send(z_two.at[n, order, i], z_in.at[n, order, 2 + i], gx=dest)
+                    net.send(z_two.at[n, order, i], z_in.at[n, order, 2 + i], gx=z_at(2 * d))
                 )
 
         def collect(self, order):
             n = self.n
             for copy in self.last_hops[order]:
                 copy.wait_recv()
-            value = keep[n, order, z]
+            value = keep[n, order, 0]
             for s in range(4):
                 value = value + z_in[n, order, s].astype(F32)
             total[n, order] = value
@@ -506,50 +540,60 @@
             self.last.wait_recv()
             return total[self.n, self.here] + ty_in[self.n].astype(F32)
 
-    ys = FeatureSum(0, lambda k, cols: dot(act_all[rows_of(k), :], w_full[cols, :], 1, 1))
-    norms = FeatureSum(1, lambda k, cols: dot(pg_all[rows_of(k), :], w_in[cols, :], 1, 1))
+    ys = FeatureSum(0, lambda k, cols: dot(both_halves(act_all, k), w_full[cols, :], 1, 1))
+    norms = FeatureSum(1, lambda k, cols: dot(both_halves(pg_all, k), w_in[cols, :], 1, 1))
 
     STEP = 32
-    for part_index in range(2):
-        pres.pairs[part_index].wait_recv()
-
-        def activate(i, carry):
-            start = pl.multiple_of(part_index * HALF + i * STEP, STEP)
+
+    def activate(half):
+        pres[half].pair.wait_recv()
+
+        def one(i, carry):
+            start = pl.multiple_of(i * STEP, STEP)
             rows = pl.ds(start, STEP)
-            v = pres.total(rows) + bias
+            v = pres[half].total(rows) + bias
             t = jnp.tanh(ROOT * (v + CUBIC * v * v * v))
-            act_all[pl.ds(pl.multiple_of(mine + start, STEP), STEP), :] = (
-                0.5 * v * (1.0 + t)
-            ).astype(BF)
-            pre[rows, :] = 0.5 * (1.0 + t) + 0.5 * v * (1.0 - t * t) * ROOT * (
+            place = pl.multiple_of(half * (4 * HALF) + x * HALF + start, STEP)
+            act_all[pl.ds(place, STEP), :] = (0.5 * v * (1.0 + t)).astype(BF)
+            pre[half, rows, :] = 0.5 * (1.0 + t) + 0.5 * v * (1.0 - t * t) * ROOT * (
                 1.0 + 3.0 * CUBIC * v * v
             )
             return carry
 
-        lax.fori_loop(0, HALF // STEP, activate, 0)
-    acts = HiddenGather(act_all)
-
-    grads.pair_up()
-    acts.onward()
-    ys.products(0)
-    for part_index in range(2):
-        grads.pairs[part_index].wait_recv()
-
-        def backward(i, carry):
-            start = pl.multiple_of(part_index * HALF + i * STEP, STEP)
+        lax.fori_loop(0, HALF // STEP, one, 0)
+        acts.begin(half)
+
+    def backward(half):
+        grads[half].pair.wait_recv()
+
+        def one(i, carry):
+            start = pl.multiple_of(i * STEP, STEP)
             rows = pl.ds(start, STEP)
-            pg_all[pl.ds(pl.multiple_of(mine + start, STEP), STEP), :] = (
-                grads.total(rows) * pre[rows, :]
+            place = pl.multiple_of(half * (4 * HALF) + x * HALF + start, STEP)
+            pg_all[pl.ds(place, STEP), :] = (
+                grads[half].total(rows) * pre[half, rows, :]
             ).astype(BF)
             return carry
 
-        lax.fori_loop(0, HALF // STEP, backward, 0)
-    pgs = HiddenGather(pg_all)
-
+        lax.fori_loop(0, HALF // STEP, one, 0)
+        pgs.begin(half)
+
+    pres[1].pair_up()
+    activate(0)
+    grads[0].relayed()
+    grads[1].begin()
+    grads[0].pair_up()
+    activate(1)
+    grads[1].relayed()
+    backward(0)
+    grads[1].pair_up()
+    acts.onward()
+    acts.neighbours()
+    ys.products(0)
+    backward(1)
     ys.scatter(0)
     acts.finish()
     ys.products(1)
-    ys.relay(0)
 
     def w_out_tile(rows):
         w_send[rows, :] = dot(cot_all[:, rows], act_all[...], 0, 0).astype(BF)
@@ -560,8 +604,10 @@
             w_send.at[features_of(g_at(s))], w_out_grad.at[:, hidden_of(g)], gy=g_at(s)
         )
     net.local(w_send.at[features_of(g)], w_out_grad.at[:, hidden_of(g)])
+    pgs.onward()
+    ys.relay(0)
     ys.scatter(1)
-    pgs.onward()
+    pgs.neighbours()
     norms.products(0)
     ys.relay(1)
     norms.scatter(0)
@@ -590,20 +636,30 @@
     norms.collect(0)
     norms.collect(1)
     norms.exchange()
-    gz_in[z] = sum(
-        jnp.sum(total[1, order] * rows_centred(norms.target(order)), 0, keepdims=True)
-        for order in range(2)
-    )
+    partial = jnp.zeros((1, W), F32)
+    for order in range(2):
+        value = total[1, order]
+        centred = centred_rows(norms.target(order), c, z)
+        partial = partial + jnp.sum(value * centred, 0, keepdims=True)
+        value = value * gain_row()
+        stat2_out[order] = pack(
+            jnp.sum(value, 1, keepdims=True), jnp.sum(value * centred, 1, keepdims=True)
+        )
+    mine, other = norms.here, 1 - norms.here
+    stats2 = [
+        net.send(stat2_out.at[mine], stat2_in.at[s], gz=q_at(s)) for s in range(1, NZ)
+    ] + [
+        net.send(stat2_out.at[other], stat2_in.at[NZ + s], gy=y_peer, gz=q_at(s))
+        for s in range(NZ)
+    ]
+    stat2_in[0] = stat2_out[mine]
+    gz_in[z] = partial
     gains = [net.send(gz_in.at[z], gz_in.at[z], gx=z_at(s)) for s in range(1, NZ)]
     y_out[...] = ys.result().astype(BF)
 
     norm_grad = norms.result()
     centred = centre()
     hat_grad = norm_grad * gain_row()
-    stat2_in[0] = pair_tile(
-        jnp.sum(hat_grad, 1, keepdims=True), jnp.sum(hat_grad * centred, 1, keepdims=True)
-    )
-    stats2 = [net.send(stat2_in.at[0], stat2_in.at[s], gz=q_at(s)) for s in range(1, NZ)]
     for copy in gains:
         copy.wait_recv()
     value = gz_in[0]
@@ -613,10 +669,10 @@
     gains = [net.send(gy_in.at[g], gy_in.at[g], gy=g_at(s)) for s in range(1, 4)]
     for copy in stats2:
         copy.wait_recv()
-    both = stat2_in[0]
-    for s in range(1, NZ):
-        both = both + stat2_in[s]
-    first, second = split_pair(both)
+    packed = stat2_in[0]
+    for s in range(1, 2 * NZ):
+        packed = packed + stat2_in[s]
+    first, second = unpack(packed)
     in_grad[...] = (
         (hat_grad - first / FEATURES - centred * (second / FEATURES)) * inv_std
     ).astype(BF)
@@ -670,15 +726,15 @@
             pltpu.VMEM((W, W), BF),
             pltpu.VMEM((NZ, SH, LANES), F32),
             pltpu.VMEM((4, NZ, 1, LANES), F32),
-            pltpu.VMEM((2, CH, W), BF),
-            pltpu.VMEM((2, 2, HALF, W), F32),
-            pltpu.VMEM((2, 2, CH, W), BF),
-            pltpu.VMEM((2, CH, W), F32),
-            pltpu.VMEM((2, 2, HALF, W), BF),
-            pltpu.VMEM((2, 2, CH, W), BF),
-            pltpu.VMEM((2, CH, W), BF),
-            pltpu.VMEM((2, CH, W), BF),
-            pltpu.VMEM((CH, W), F32),
+            pltpu.VMEM((4, HALF, W), BF),
+            pltpu.VMEM((4, 2, QUART, W), F32),
+            pltpu.VMEM((4, 2, HALF, W), BF),
+            pltpu.VMEM((4, HALF, W), F32),
+            pltpu.VMEM((4, 2, QUART, W), BF),
+            pltpu.VMEM((4, 2, HALF, W), BF),
+            pltpu.VMEM((4, HALF, W), BF),
+            pltpu.VMEM((4, HALF, W), BF),
+            pltpu.VMEM((2, HALF, W), F32),
             pltpu.VMEM((2, 2, NZ, SH, W), F32),
             pltpu.VMEM((2, 2, NZ, SH, W), BF),
             pltpu.VMEM((2, 2, NZ, SH, W), BF),
@@ -690,7 +746,8 @@
             pltpu.VMEM((2, 2, SH, W), F32),
             pltpu.VMEM((2, SH, W), BF),
             pltpu.VMEM((2, SH, W), BF),
-            pltpu.VMEM((NZ, SH, LANES), F32),
+            pltpu.VMEM((2 * NZ, 1, LANES), F32),
+            pltpu.VMEM((2, 1, LANES), F32),
             pltpu.VMEM((NZ, 1, W), F32),
             pltpu.VMEM((4, 1, W), F32),
             pltpu.SemaphoreType.DMA((COPIES,)),

time: 107 us -> 105 us (0.981)
  Pallas kernels: 106 us -> 104 us
    pallas_call x1, Pallas kernels: 102 us -> 99.7 us  [shards(): pl.pallas_call(kernel, out_shape=results, in_specs=[vmem, vmem, hbm, vmem...]
where the time goes in v4:
time: 105 us; the launch traced here: 104 us
  Pallas kernels  104 us (99%)
    pallas_call x1, Pallas kernels, shards(): pl.pallas_call(kernel, out_shape=results, in_specs=[vmem, vmem, hbm, vmem...  99.7 us
    pallas_call x1, Pallas kernels, shards(): pl.pallas_call(hand_over, out_shape=results[:5] + (jax.ShapeDtypeStruct((...  4.03 us

profile of v4, /device:TPU:1, one launch (start us, length us, event | category | flops | bytes accessed | tf_op | source)
XLA Modules:
  0.0 104.4 jit_solution(18117321337891951514)
XLA Ops:
  0.6 99.7 %shard_map.109 = (bf16[24,768]{1,0:T(8,128)(2,1)}, bf16[24,768]{1,0:T(8,128)(2,1)}, bf16[768,768]{1,0:T(8,128)(2,1)}, bf16[192,3072]{1,0:T(8,128)(2,1)}, f32[4,1,768]{2,1,0:T(1,128)}, /*index=5*/f32[1,768]{1,0:T(1,128)}) custom-call(bf16[24,768]{1,0:T(8,128)(2,1)} %tok.1, f32[768]{0:T(1024)} %gain.1, bf16[768,768]{1,0:T(8,128)(2,1)} %w_in_hbm.1, ...), custom_call_target="tpu_custom_call" | custom-call | flops 5435817984 | bytes 5898240 | tf_op jit(solution)/shard_map/pallas_call | solution.py:711
  100.3 4.0 %shard_map.110 = (bf16[24,768]{1,0:T(8,128)(2,1)}, bf16[24,768]{1,0:T(8,128)(2,1)}, bf16[768,768]{1,0:T(8,128)(2,1)}, bf16[192,3072]{1,0:T(8,128)(2,1)}, f32[4,1,768]{2,1,0:T(1,128)}, /*index=5*/f32[768]{0:T(1024)}) custom-call(bf16[24,768]{1,0:T(8,128)(2,1)} %get-tuple-element.18.refs_0_, bf16[24,768]{1,0:T(8,128)(2,1)} %get-tuple-element.19.refs_1_, ...), custom_call_target="tpu_custom_call" | custom-call | tf_op jit(solution)/shard_map/pallas_call | solution.py:764

commit v5 on v4

--- a/solution.py
+++ b/solution.py
@@ -609,30 +609,30 @@
     ys.scatter(1)
     pgs.neighbours()
     norms.products(0)
+    norms.scatter(0)
     ys.relay(1)
-    norms.scatter(0)
+    pgs.finish()
+    norms.products(1)
+    norms.scatter(1)
+    norms.relay(0)
+
+    def bias_sum(i, carry):
+        rows = pl.ds(pl.multiple_of(i * STEP, STEP), STEP)
+        return carry + jnp.sum(pg_all[rows, :].astype(F32), 0, keepdims=True)
+
+    b_grad[g] = lax.fori_loop(0, W // STEP, bias_sum, jnp.zeros((1, W), F32))
+    biases = [net.send(b_grad.at[g], b_grad.at[g], gy=g_at(s)) for s in range(1, 4)]
+
+    def w_in_tile(rows):
+        w_in_out[rows, :] = dot(nor_all[:, rows], pg_all[...], 0, 0).astype(BF)
+
+    tiles(w_in_tile)
+    net.local(w_in_out, w_in_grad)
+
+    norms.relay(1)
     ys.collect(0)
     ys.collect(1)
     ys.exchange()
-    pgs.finish()
-    norms.products(1)
-    norms.relay(0)
-    norms.scatter(1)
-
-    def bias_sum(i, carry):
-        rows = pl.ds(pl.multiple_of(i * STEP, STEP), STEP)
-        return carry + jnp.sum(pg_all[rows, :].astype(F32), 0, keepdims=True)
-
-    b_grad[g] = lax.fori_loop(0, W // STEP, bias_sum, jnp.zeros((1, W), F32))
-    biases = [net.send(b_grad.at[g], b_grad.at[g], gy=g_at(s)) for s in range(1, 4)]
-
-    def w_in_tile(rows):
-        w_in_out[rows, :] = dot(nor_all[:, rows], pg_all[...], 0, 0).astype(BF)
-
-    tiles(w_in_tile)
-    net.local(w_in_out, w_in_grad)
-
-    norms.relay(1)
     norms.collect(0)
     norms.collect(1)
     norms.exchange()

time: 105 us -> 100 us (0.952)
  Pallas kernels: 104 us -> 99.2 us
    pallas_call x1, Pallas kernels: 99.7 us -> 95.2 us  [shards(): pl.pallas_call(kernel, out_shape=results, in_specs=[vmem, vmem, hbm, vmem...]
where the time goes in v5:
time: 100 us; the launch traced here: 99.8 us
  Pallas kernels  99.2 us (99%)
    pallas_call x1, Pallas kernels, shards(): pl.pallas_call(kernel, out_shape=results, in_specs=[vmem, vmem, hbm, vmem...  95.2 us
    pallas_call x1, Pallas kernels, shards(): pl.pallas_call(hand_over, out_shape=results[:5] + (jax.ShapeDtypeStruct((...  4.03 us

profile of v5, /device:TPU:1, one launch (start us, length us, event | category | flops | bytes accessed | tf_op | source)
XLA Modules:
  0.0 99.8 jit_solution(59505599058738823)
XLA Ops:
  0.6 95.2 %shard_map.109 = (bf16[24,768]{1,0:T(8,128)(2,1)}, bf16[24,768]{1,0:T(8,128)(2,1)}, bf16[768,768]{1,0:T(8,128)(2,1)}, bf16[192,3072]{1,0:T(8,128)(2,1)}, f32[4,1,768]{2,1,0:T(1,128)}, /*index=5*/f32[1,768]{1,0:T(1,128)}) custom-call(bf16[24,768]{1,0:T(8,128)(2,1)} %tok.1, f32[768]{0:T(1024)} %gain.1, bf16[768,768]{1,0:T(8,128)(2,1)} %w_in_hbm.1, ...), custom_call_target="tpu_custom_call" | custom-call | flops 5435817984 | bytes 5898240 | tf_op jit(solution)/shard_map/pallas_call | solution.py:711
  95.8 4.0 %shard_map.110 = (bf16[24,768]{1,0:T(8,128)(2,1)}, bf16[24,768]{1,0:T(8,128)(2,1)}, bf16[768,768]{1,0:T(8,128)(2,1)}, bf16[192,3072]{1,0:T(8,128)(2,1)}, f32[4,1,768]{2,1,0:T(1,128)}, /*index=5*/f32[768]{0:T(1024)}) custom-call(bf16[24,768]{1,0:T(8,128)(2,1)} %get-tuple-element.18.refs_0_, bf16[24,768]{1,0:T(8,128)(2,1)} %get-tuple-element.19.refs_1_, ...), custom_call_target="tpu_custom_call" | custom-call | tf_op jit(solution)/shard_map/pallas_call | solution.py:764
